TPU v7x, 256 devices: a whole 4x4x8 slice. The times are simulated.
256 devices in a mesh: ctx: 8 (over y_lo, x), exp: 32 (over z, y_hi, core).
Axes of the slice: x: 4, y: 4 (y_hi: 2, y_lo: 2; y = y_hi * 2 + y_lo), z: 8, core: 2. Of those that a mesh axis runs over, the one named last changes fastest.
Arguments:
- queries: bfloat16 [32, 1024, 4096], P('exp', 'ctx'), may hold values from -48 to 48
- keys: bfloat16 [32, 1024, 256], P('exp', 'ctx'), may hold values from -4 to 4
- values: bfloat16 [32, 1024, 256], P('exp', 'ctx'), may hold values from -6 to 6
- positions: int32 [32, 1024], P('exp', 'ctx'), may hold values from 0 to 65535, as said below
- residual: bfloat16 [32, 1024, 4096], P('exp', 'ctx'), may hold values from -6 to 6
- norm_gain: float32 [4096], replicated, may hold values from 0.25 to 1.75
- expert_ids: int32 [32, 1024, 8], P('exp', 'ctx'), may hold values from 0 to 127, as said below
- route_weights: float32 [32, 1024, 8], P('exp', 'ctx'), may hold values from 0.3 to 1
- w_gate: bfloat16 [32, 4096, 1536], P('exp', None, 'ctx'), may hold values from -0.09375 to 0.09375
- w_up: bfloat16 [32, 4096, 1536], P('exp', None, 'ctx'), may hold values from -0.09375 to 0.09375
- w_down: bfloat16 [32, 1536, 4096], P('exp', None, 'ctx'), may hold values from -0.15625 to 0.15625
Outputs:
- layer_out: bfloat16 [32, 1024, 4096], P('exp', 'ctx')
Inputs may be any that keep to these rules, and one draw needn't show every extreme that they name: `positions`: strictly increasing along each sequence. `expert_ids`: A token's 8 ids differ. In each aligned block of 128 tokens of a sequence no id is named by more than 9 tokens.
All inputs are finite; a program needn't handle non-finite values.
Results may differ from a plain program's by a relative error of at most 0.007.
Values may be sent and summed in bfloat16 or wider, within the bound.
No kernel may reach another device: no remote copies, remote signals or barrier semaphores. Data moves between devices by JAX's collectives and lax.ppermute only.
A program may use at most 128 MiB of HBM per device.

v0:
```python
import math

import jax
import jax.numpy as jnp
from jax import lax
from jax.sharding import PartitionSpec as P

HEADS = 32
KV_HEADS = 2
HEAD_DIM = 128
ROUTED = 128
TOP = 8


def yarn_tables(position_values):
    half = HEAD_DIM // 2
    theta_base = 1000000.0
    factor = 4.0
    trained_span = 32768.0

    def bound_dim(turns):
        return (
            HEAD_DIM * math.log(trained_span / (turns * 2 * math.pi)) / (2 * math.log(theta_base))
        )

    lower = max(math.floor(bound_dim(32.0)), 0)
    upper = min(math.ceil(bound_dim(1.0)), HEAD_DIM - 1)
    pair_index = jnp.arange(half, dtype=jnp.float32)
    extrapolated = jnp.exp(-(2.0 * pair_index / HEAD_DIM) * math.log(theta_base))
    ramp = jnp.clip((pair_index - lower) / max(upper - lower, 1), 0.0, 1.0)
    inverse = extrapolated / factor * ramp + extrapolated * (1.0 - ramp)
    magnitude = 0.1 * math.log(factor) + 1.0
    angles = position_values.astype(jnp.float32)[..., None] * inverse
    return (jnp.cos(angles) * magnitude, jnp.sin(angles) * magnitude)


def rotate_heads(field, cosine, sine):
    half = HEAD_DIM // 2
    first = field[..., :half]
    second = field[..., half:]
    return jnp.concatenate(
        [first * cosine - second * sine, second * cosine + first * sine], axis=-1
    )


def per_device(
    queries,
    keys,
    values,
    positions,
    residual,
    norm_gain,
    expert_ids,
    route_weights,
    w_gate,
    w_up,
    w_down,
):
    tokens_here = queries.shape[1]
    width = queries.shape[2]
    group = HEADS // KV_HEADS
    cosine, sine = yarn_tables(positions[0])
    cosine = cosine[:, None, :]
    sine = sine[:, None, :]
    q_rot = rotate_heads(
        queries[0].reshape(tokens_here, HEADS, HEAD_DIM).astype(jnp.float32), cosine, sine
    ).astype(jnp.bfloat16)
    k_rot = rotate_heads(
        keys[0].reshape(tokens_here, KV_HEADS, HEAD_DIM).astype(jnp.float32), cosine, sine
    ).astype(jnp.bfloat16)
    grouped = jnp.transpose(q_rot.reshape(tokens_here, KV_HEADS, group, HEAD_DIM), (1, 2, 0, 3))
    grouped = grouped.reshape(KV_HEADS, group * tokens_here, HEAD_DIM)
    stacked = jnp.stack([k_rot.reshape(tokens_here, KV_HEADS * HEAD_DIM), values[0]])
    my_block = lax.axis_index("ctx")
    query_index = my_block * tokens_here + jnp.arange(tokens_here, dtype=jnp.int32)
    last_query = my_block * tokens_here + tokens_here - 1
    inv_root = 1.0 / math.sqrt(HEAD_DIM)
    initial = (
        jnp.full((KV_HEADS, group, tokens_here), -1e30, jnp.float32),
        jnp.zeros((KV_HEADS, group, tokens_here), jnp.float32),
        jnp.zeros((KV_HEADS, group, tokens_here, HEAD_DIM), jnp.float32),
    )
    piece = lax.all_gather(stacked, "ctx", axis=1, tiled=True)
    count = piece.shape[1]

    def take_block(held):
        running_max, running_total, mixed = held
        key_heads = piece[0].reshape(count, KV_HEADS, HEAD_DIM)
        value_heads = piece[1].reshape(count, KV_HEADS, HEAD_DIM)
        scores = (
            jnp.einsum("kmd,nkd->kmn", grouped, key_heads, preferred_element_type=jnp.float32)
            * inv_root
        )
        key_index = jnp.arange(count, dtype=jnp.int32)
        masking = jnp.where(
            key_index[None, :] <= query_index[:, None], jnp.float32(0.0), jnp.float32(-1e30)
        )
        scores = scores.reshape(KV_HEADS, group, tokens_here, count) + masking
        new_max = jnp.maximum(running_max, jnp.max(scores, axis=-1))
        weight = jnp.exp(scores - new_max[..., None])
        running_total = jnp.sum(weight, axis=-1)
        added = jnp.einsum(
            "kgtn,nkd->kgtd",
            weight.astype(jnp.bfloat16),
            value_heads,
            preferred_element_type=jnp.float32,
        )
        mixed = added
        return (new_max, running_total, mixed)

    state = lax.cond(jnp.int32(0) <= last_query, take_block, lambda held: held, initial)
    attn_heads = state[2] / state[1][..., None]
    attn = jnp.transpose(attn_heads, (2, 0, 1, 3)).reshape(tokens_here, width)
    h_state = residual[0].astype(jnp.float32) + attn
    mean_square = jnp.mean(h_state * h_state, axis=-1, keepdims=True)
    normed = (h_state / jnp.sqrt(mean_square + 1e-06) * norm_gain).astype(jnp.bfloat16)
    owners = lax.axis_size("exp")
    ctx_count = lax.axis_size("ctx")
    capacity = tokens_here * TOP // ROUTED + 1
    slot_count = owners * capacity
    flat_ids = expert_ids[0].reshape(-1)
    flat_weights = route_weights[0].reshape(-1)
    in_window = flat_ids < owners
    onehot = (flat_ids[:, None] == jnp.arange(owners, dtype=jnp.int32)[None, :]).astype(jnp.int32)
    before = jnp.cumsum(onehot, axis=0) - onehot
    rank = jnp.sum(before * onehot, axis=1)
    slot = jnp.where(in_window, flat_ids * capacity + rank, -1)
    member = slot[:, None] == jnp.arange(slot_count, dtype=jnp.int32)[None, :]
    selector = jnp.any(member.reshape(tokens_here, TOP, slot_count), axis=1).astype(jnp.bfloat16)
    weighted = jnp.sum(
        jnp.where(member, flat_weights[:, None], jnp.float32(0.0)).reshape(
            tokens_here, TOP, slot_count
        ),
        axis=1,
    )
    outgoing = jnp.einsum("ts,td->sd", selector, normed, preferred_element_type=jnp.float32).astype(
        jnp.bfloat16
    )
    outgoing = outgoing.reshape(owners, capacity, width)
    gate_local = w_gate[0]
    up_local = w_up[0]
    down_local = w_down[0]
    arrived = lax.all_to_all(outgoing, "exp", split_axis=0, concat_axis=0, tiled=True)
    hidden_piece = lax.all_gather(
        arrived.reshape(owners * capacity, width), "ctx", axis=0, tiled=True
    )
    gate = jnp.dot(hidden_piece, gate_local, preferred_element_type=jnp.float32)
    upper = jnp.dot(hidden_piece, up_local, preferred_element_type=jnp.float32)
    act_part = (jax.nn.silu(gate) * upper).astype(jnp.bfloat16)
    act_full = lax.all_gather(act_part, "ctx", axis=1, tiled=True)
    out_cols = jnp.dot(act_full, down_local, preferred_element_type=jnp.float32).astype(
        jnp.bfloat16
    )
    out_cols = out_cols.reshape(ctx_count, owners, capacity, out_cols.shape[1])
    returned = lax.all_to_all(
        lax.all_to_all(out_cols, "ctx", split_axis=0, concat_axis=3, tiled=True),
        "exp",
        split_axis=1,
        concat_axis=0,
        tiled=True,
    )
    returned = returned.reshape(slot_count, width)
    moe_sum = jnp.dot(
        weighted,
        returned.astype(jnp.float32),
        precision=lax.Precision.HIGHEST,
        preferred_element_type=jnp.float32,
    )
    return (h_state + moe_sum).astype(jnp.bfloat16)[None]


def solution(mesh):
    return jax.shard_map(
        per_device,
        mesh=mesh,
        in_specs=(
            P("exp", "ctx", None),
            P("exp", "ctx", None),
            P("exp", "ctx", None),
            P("exp", "ctx"),
            P("exp", "ctx", None),
            P(),
            P("exp", "ctx", None),
            P("exp", "ctx", None),
            P("exp", None, "ctx"),
            P("exp", None, "ctx"),
            P("exp", None, "ctx"),
        ),
        out_specs=P("exp", "ctx", None),
        check_vma=False,
    )
```

profile of v0, /device:TPU:17, one launch (start us, length us, event | category | flops | bytes accessed | tf_op | source)
XLA Modules:
  0.0 672.5 jit_solution(14455704421072768703)
XLA Ops:
  6.6 0.8 convert_bitcast_fusion.3
  7.4 0.9 copy.85
  8.3 1.0 copy.67
  9.3 0.2 fusion.23
  9.5 0.7 pad_maximum_fusion
  10.5 0.8 copy.69
  11.4 0.2 convert_bitcast_fusion.2
  11.7 1.7 copy.91
  13.4 0.2 convert_bitcast_fusion
  13.6 1.7 copy.94
  15.3 9.0 %reduce-window.6 = s32[32,8,128]{2,1,0:T(8,128)S(1)} reduce-window(s32[32,8,128]{2,1,0:T(8,128)S(1)} %fusion.21, s32[]{:T(128)} %constant.18.clone.1), window={size=1x1x128 pad=0_0x0_0x127_0}, to_apply=%region_4.5 | reduce-window | flops 4161536 | bytes 262148 | tf_op jit(solution)/shard_map/reduce-window
  24.4 0.1 copy.73
  24.7 0.1 broadcast_add_fusion.1
  25.0 0.2 fusion.15
  25.2 3.0 fusion.31
  28.1 2.4 subtract_convert_fusion
  30.6 1.6 maximum_bitcast_fusion
  32.1 17.1 %all-gather.4.cloned.1.call-done = bf16[2,1024,256]{1,2,0:T(8,128)(2,1)} async-done(((bf16[2,128,256]{1,2,0:T(8,128)(2,1)}), bf16[2,1024,256]{1,2,0:T(8,128)(2,1)}) %all-gather.4.cloned.1.call-update) | async-done | bytes 1048592 | tf_op jit(solution)/shard_map/all_gather | solution.py:83
  49.2 24.8 %conditional.1 = (f32[2,16,128]{2,1,0:T(8,128)S(1)}, f32[2,16,128,128]{3,2,1,0:T(8,128)S(1)}) conditional(s32[]{:T(128)} %convert_element_type.79, () %tuple.13, (bf16[2,16,128,128]{3,2,1,0:T(8,128)(2,1)}, bf16[2,1024,256]{1,2,0:T(8,128)(2,1)}, s32[]{:T(128)}, s32[128]{0:T(128)S(1)}) %tuple.14), branch_computations={%region_0.1_spmd, %region_1.4_spmd} | conditional | flops 2185490432 | bytes 91932240 | solution.py:111
  49.2 0.1 fusion.3
  49.3 1.1 add.63
  50.4 0.1 copy-done.5
  50.6 1.0 copy-done.3
  51.7 7.0 %add_reduce_fusion = (f32[2,2048]{1,0:T(2,128)S(1)}, f32[2,2048,1024]{2,1,0:T(8,128)}) fusion(f32[2048,1024]{1,0:T(8,128)S(1)} %bitcast.108, bf16[2,2048,128]{2,1,0:T(8,128)(2,1)S(1)} %bitcast.116, bf16[1024,2,128]{0,2,1:T(8,128)(2,1)S(1)} %bitcast.119), kind=kOutput, calls=%fused_computation.2 | convolution fusion | flops 1086320640 | bytes 26755072 | tf_op jit(solution)/shard_map/cond/branch_1_fun/kmd,nkd->kmn/dot_general | solution.py:91
  58.7 7.4 %fusion = f32[2,16,128,128]{3,2,1,0:T(8,128)S(1)} fusion(bf16[1024,2,128,1]{0,2,3,1:T(8,128)(2,1)S(1)} %bitcast.122, f32[2,16,128,1024]{3,2,1,0:T(8,128)} %bitcast.110, f32[2,16,128]{2,1,0:T(8,128)S(1)} %bitcast.127, f32[128,1024]{1,0:T(8,128)S(1)} %fusion.3), kind=kOutput, calls=%fused_computation.3 | convolution fusion | flops 1086324736 | bytes 19939328 | tf_op jit(solution)/shard_map/cond/branch_1_fun/kgtn,nkd->kgtd/dot_general | solution.py:102
  66.1 7.9 %exponential_reduce_fusion = f32[2,2048]{1,0:T(2,128)S(1)} fusion(f32[2,2048,1024]{2,1,0:T(8,128)} %get-tuple-element.31, f32[2,2048]{1,0:T(2,128)S(1)} %get-tuple-element.29, f32[2048,1024]{1,0:T(8,128)S(1)} %bitcast.109), kind=kLoop, calls=%fused_computation.1 | loop fusion | flops 12578816 | bytes 25198592 | tf_op jit(solution)/shard_map/cond/branch_1_fun/reduce_sum | solution.py:101
  74.0 3.0 fusion.10
  77.0 1.2 copy.68
  78.2 1.3 copy-done.1
  79.5 3.1 convolution_convert_fusion
  82.6 4.6 reshape.226
  87.2 110.1 %all_to_all.32 = bf16[32,9,4096]{2,1,0:T(8,128)(2,1)} all-to-all(bf16[32,9,4096]{2,1,0:T(8,128)(2,1)} %reshape.226), channel_id=1, replica_groups=mesh['ctx'=8,'exp'=32] {'exp'}, dimensions={0} | all-to-all | bytes 4718592 | tf_op jit(solution)/shard_map/all_to_all | solution.py:143
  197.3 4.7 reshape.227
  202.1 189.3 %all-gather.6.cloned.1.call-done = bf16[2304,4096]{1,0:T(8,128)(2,1)} async-done(((bf16[288,4096]{1,0:T(8,128)(2,1)}), bf16[2304,4096]{1,0:T(8,128)(2,1)}) %all-gather.6.cloned.1.call-update) | async-done | bytes 18874384 | tf_op jit(solution)/shard_map/all_gather | solution.py:144
  391.4 12.6 %fusion.13 = f32[2304,192]{0,1:T(8,128)S(1)} fusion(bf16[2304,4096]{1,0:T(8,128)(2,1)} %all-gather.6.cloned.1.call-done, bf16[1,4096,192]{1,2,0:T(8,128)(2,1)} %param.21), kind=kOutput, calls=%fused_computation.34 | convolution fusion | flops 3623878656 | bytes 22216704 | tf_op jit(solution)/shard_map/dot_general | solution.py:147
  404.1 7.3 %fusion.7 = bf16[2304,192]{0,1:T(8,128)(2,1)} fusion(bf16[2304,4096]{1,0:T(8,128)(2,1)S(1)} %copy-done.7, f32[2304,192]{0,1:T(8,128)S(1)} %fusion.13, bf16[1,4096,192]{1,2,0:T(8,128)(2,1)S(1)} %copy-done.8), kind=kOutput, calls=%fused_computation.20 | convolution fusion | flops 3626532864 | bytes 23101440 | tf_op jit(solution)/shard_map/dot_general | solution.py:148
  411.4 81.2 %all-gather.8.cloned.1.call-done = bf16[2304,1536]{0,1:T(8,128)(2,1)} async-done(((bf16[2304,192]{0,1:T(8,128)(2,1)}), bf16[2304,1536]{0,1:T(8,128)(2,1)}) %all-gather.8.cloned.1.call-update) | async-done | bytes 7077904 | tf_op jit(solution)/shard_map/all_gather | solution.py:150
  492.6 8.2 %convolution_convert_fusion.1 = bf16[2304,512]{1,0:T(8,128)(2,1)} fusion(bf16[2304,1536]{0,1:T(8,128)(2,1)} %all-gather.8.cloned.1.call-done, bf16[1,1536,512]{2,1,0:T(8,128)(2,1)S(1)} %copy-done), kind=kOutput, calls=%fused_computation.18 | convolution fusion | flops 3625058304 | bytes 11010048 | tf_op jit(solution)/shard_map/dot_general | solution.py:151
  500.8 5.3 reshape.228
  506.1 3.7 copy.77
  509.8 31.4 %all_to_all.33 = bf16[8,32,9,512]{3,1,2,0:T(8,128)(2,1)S(1)} all-to-all(bf16[8,32,9,512]{3,1,2,0:T(8,128)(2,1)S(1)} %copy.77), channel_id=1, replica_groups=mesh['ctx'=8,'exp'=32] {'ctx'}, dimensions={0} | all-to-all | bytes 4718592 | tf_op jit(solution)/shard_map/all_to_all | solution.py:156
  541.2 2.7 copy.84
  543.9 5.5 reshape.235
  549.5 11.7 %all-to-all-start.2 = ((bf16[1,32,9,4096]{3,2,0,1:T(8,128)(2,1)}), bf16[1,32,9,4096]{3,2,0,1:T(8,128)(2,1)}, u32[]{:S(2)}, u32[]{:S(2)}) async-start(bf16[1,32,9,4096]{3,2,0,1:T(8,128)(2,1)} %reshape.235), calls=%async_computation.2 | async-start | bytes 8388608 | tf_op jit(solution)/shard_map/all_to_all | solution.py:155
  561.2 0.1 select_reduce_fusion
  561.4 93.8 %all-to-all-done.2 = bf16[1,32,9,4096]{3,2,0,1:T(8,128)(2,1)} async-done(((bf16[1,32,9,4096]{3,2,0,1:T(8,128)(2,1)}), bf16[1,32,9,4096]{3,2,0,1:T(8,128)(2,1)}, u32[]{:S(2)}, u32[]{:S(2)}) %all-to-all-start.2) | async-done | bytes 2359328 | tf_op jit(solution)/shard_map/all_to_all | solution.py:155
  655.2 4.7 reshape.229
  659.9 6.1 fusion.6
  (46 shorter events, 1.1 us)
Async XLA Ops:
  6.5 486.1 %copy-start = (bf16[1,1536,512]{2,1,0:T(8,128)(2,1)S(1)}, bf16[1,1536,512]{2,1,0:T(8,128)(2,1)}, u32[]{:S(2)}) copy-start(bf16[1,1536,512]{2,1,0:T(8,128)(2,1)} %param.23) | copy-start | bytes 4718596
  6.5 4.9 copy-start.4
  6.5 42.7 %all-gather.4.cloned.1.call-start = ((), (), s32[]{:S(2)}) async-start(), calls=%async_computation.3 | async-start | bytes 1179648 | tf_op jit(solution)/shard_map/all_gather | solution.py:83
  10.2 381.2 %all-gather.6.cloned.1.call-start = ((), (), s32[]{:S(2)}) async-start(), calls=%async_computation.4 | async-start | bytes 21233664 | tf_op jit(solution)/shard_map/all_gather | solution.py:144
  11.7 1.7 copy-start.2
  49.3 1.2 copy-start.5
  50.4 1.3 copy-start.3
  77.0 2.6 copy-start.9
  78.2 1.3 copy-start.1
  202.0 290.5 %all-gather.8.cloned.1.call-start = ((), (), s32[]{:S(2)}) async-start(), calls=%async_computation.5 | async-start | bytes 7962624 | tf_op jit(solution)/shard_map/all_gather | solution.py:150
  391.4 12.7 %copy-start.7 = (bf16[2304,4096]{1,0:T(8,128)(2,1)S(1)}, bf16[2304,4096]{1,0:T(8,128)(2,1)}, u32[]{:S(2)}) copy-start(bf16[2304,4096]{1,0:T(8,128)(2,1)} %all-gather.6.cloned.1.call-done) | copy-start | bytes 56623108
  391.4 12.7 %copy-start.8 = (bf16[1,4096,192]{1,2,0:T(8,128)(2,1)S(1)}, bf16[1,4096,192]{1,2,0:T(8,128)(2,1)}, u32[]{:S(2)}) copy-start(bf16[1,4096,192]{1,2,0:T(8,128)(2,1)} %param.22) | copy-start | bytes 4718596
  549.5 11.7 %copy-start.6 = (f32[1,128,8]{1,2,0:T(8,128)S(1)}, f32[1,128,8]{1,2,0:T(8,128)}, u32[]{:S(2)}) copy-start(f32[1,128,8]{1,2,0:T(8,128)} %param.20) | copy-start | bytes 12292
  549.5 105.7 %all-to-all-start.2 = ((bf16[1,32,9,4096]{3,2,0,1:T(8,128)(2,1)}), bf16[1,32,9,4096]{3,2,0,1:T(8,128)(2,1)}, u32[]{:S(2)}, u32[]{:S(2)}) async-start(bf16[1,32,9,4096]{3,2,0,1:T(8,128)(2,1)} %reshape.235), calls=%async_computation.2 | async-start | bytes 8388608 | tf_op jit(solution)/shard_map/all_to_all | solution.py:155
Sparse Core Ops, SparseCore 0:
  10.3 38.8 all-gather.3
  202.2 189.2 all-gather.5
  411.5 81.0 all-gather.7
where the time goes:
time: 676 us; the launch traced here: 672 us
  waiting for transfers between devices  381 us (56%)
  blocking collectives  142 us (21%)
  matrix products  51.7 us (8%)
  local copies, waits for them, and re-layouts  46 us (7%)
  other arithmetic  26.6 us (4%)
  between operations  13.4 us (2%)
  starting transfers between devices  11.8 us (2%)
    all_gather x1, waiting for transfers between devices, per_device(): lax.all_gather(arrived.reshape(owners * capacity, width), 'ctx', axis=0,...  189 us
    all_to_all x1, blocking collectives, per_device(): lax.all_to_all(outgoing, 'exp', split_axis=0, concat_axis=0, tiled=True)  110 us
    all_to_all x1, waiting for transfers between devices, per_device(): lax.all_to_all(lax.all_to_all(out_cols, 'ctx', split_axis=0, concat_axis=...  93.8 us
    all_gather x1, waiting for transfers between devices, per_device(): act_full = lax.all_gather(act_part, 'ctx', axis=1, tiled=True)  81.2 us
    all_to_all x1, blocking collectives, per_device(): lax.all_to_all(out_cols, 'ctx', split_axis=0, concat_axis=3, tiled=True)  31.4 us
    all_gather x1, waiting for transfers between devices, per_device(): piece = lax.all_gather(stacked, 'ctx', axis=1, tiled=True)  17.1 us
  transfers between devices with their start and end apart: 4, of which 4 were waited for; matrix products, arithmetic and copies ran while one was open for 3% of the time, Pallas kernels for 0%

commit v1 on v0

v1 whole, which is shorter than its diff:
```python
import functools
import math

import jax
import jax.numpy as jnp
from jax import lax
from jax.experimental import pallas as pl
from jax.experimental.pallas import tpu as pltpu
from jax.sharding import Mesh
from jax.sharding import PartitionSpec as P

HEADS = 32
KV_HEADS = 2
HEAD_DIM = 128
TOP = 8
HALF = HEAD_DIM // 2
STEP_HEADS = 4
MAIN = 8

F32 = jnp.float32
BF16 = jnp.bfloat16


def yarn_tables(position_values):
    half = HEAD_DIM // 2
    theta_base = 1000000.0
    factor = 4.0
    trained_span = 32768.0

    def bound_dim(turns):
        return (
            HEAD_DIM * math.log(trained_span / (turns * 2 * math.pi)) / (2 * math.log(theta_base))
        )

    lower = max(math.floor(bound_dim(32.0)), 0)
    upper = min(math.ceil(bound_dim(1.0)), HEAD_DIM - 1)
    pair_index = jnp.arange(half, dtype=jnp.float32)
    extrapolated = jnp.exp(-(2.0 * pair_index / HEAD_DIM) * math.log(theta_base))
    ramp = jnp.clip((pair_index - lower) / max(upper - lower, 1), 0.0, 1.0)
    inverse = extrapolated / factor * ramp + extrapolated * (1.0 - ramp)
    magnitude = 0.1 * math.log(factor) + 1.0
    angles = position_values.astype(jnp.float32)[..., None] * inverse
    return (jnp.cos(angles) * magnitude, jnp.sin(angles) * magnitude)


def iota(shape, dim):
    return lax.broadcasted_iota(jnp.int32, shape, dim)


def dot(a, b):
    return jnp.dot(a, b, preferred_element_type=F32)


def rotate(head, cos2, sin2):
    return (head * cos2 + pltpu.roll(head, HALF, 1) * sin2).astype(BF16)


def params(mib):
    return pltpu.CompilerParams(vmem_limit_bytes=mib * 2**20)


def kv_kernel(k_ref, v_ref, cos_ref, sin_ref, kv_ref):
    for head in range(KV_HEADS):
        cols = slice(head * HEAD_DIM, (head + 1) * HEAD_DIM)
        kv_ref[:, cols] = rotate(k_ref[:, cols].astype(F32), cos_ref[...], sin_ref[...])
    kv_ref[:, KV_HEADS * HEAD_DIM :] = v_ref[...]


def pack_kv(keys, values, cos2, sin2):
    tokens, width = keys.shape
    return pl.pallas_call(
        kv_kernel,
        out_shape=jax.ShapeDtypeStruct((tokens, 2 * width), BF16),
        name="pack_kv",
    )(keys, values, cos2, sin2)


def slot_ranks_by_expert(ids_t, experts):
    tokens = ids_t.shape[1]
    expert = iota((experts, tokens), 0)
    named = jnp.zeros((experts, tokens), F32)
    for choice in range(TOP):
        named += (ids_t[choice : choice + 1, :] == expert).astype(F32)
    earlier = (iota((tokens, tokens), 0) < iota((tokens, tokens), 1)).astype(F32)
    rank = dot(named.astype(BF16), earlier.astype(BF16))
    return jnp.where(named > 0.5, rank, 255.0)


def attend_kernel(
    place_ref, q_ref, own_k_ref, own_v_ref, far_k_ref, far_v_ref, cos_ref, sin_ref, residual_ref,
    gain_ref, ids_ref, h_ref, rows_ref,
):
    step = pl.program_id(0)
    tokens = q_ref.shape[0]
    width = h_ref.shape[1]
    cols = STEP_HEADS * HEAD_DIM
    scale = math.log2(math.e) / math.sqrt(HEAD_DIM)
    pieces = []
    for head in range(STEP_HEADS):
        part = q_ref[:, head * HEAD_DIM : (head + 1) * HEAD_DIM].astype(F32)
        pieces.append(rotate(part, cos_ref[...], sin_ref[...]))
    q_rot = jnp.concatenate(pieces, axis=0)
    contract = (((1,), (1,)), ((), ()))
    near = lax.dot_general(q_rot, own_k_ref[...], contract, preferred_element_type=F32)
    far = lax.dot_general(q_rot, far_k_ref[...], contract, preferred_element_type=F32)
    keys = near.shape[1]
    token = iota(near.shape, 0) % tokens
    limit = place_ref[1] * tokens + token
    near = jnp.where(iota(near.shape, 1) <= limit, near, -1e30)
    far = jnp.where(place_ref[0] > 0, far, jnp.full_like(far, -1e30))
    largest = jnp.maximum(
        jnp.max(near, axis=1, keepdims=True), jnp.max(far, axis=1, keepdims=True)
    )
    near = jnp.exp2((near - largest) * scale)
    far = jnp.exp2((far - largest) * scale)
    total = jnp.sum(near, axis=1, keepdims=True) + jnp.sum(far, axis=1, keepdims=True)
    mixed = dot(near.astype(BF16), own_v_ref[...]) + dot(far.astype(BF16), far_v_ref[...])
    attn = mixed / total
    for head in range(STEP_HEADS):
        here = slice(head * HEAD_DIM, (head + 1) * HEAD_DIM)
        start = pl.multiple_of(step * cols + head * HEAD_DIM, HEAD_DIM)
        h_ref[:, pl.ds(start, HEAD_DIM)] = (
            residual_ref[:, here].astype(F32) + attn[head * tokens : (head + 1) * tokens]
        )

    @pl.when(step == pl.num_programs(0) - 1)
    def _():
        experts = rows_ref.shape[0] // MAIN
        slots = rows_ref.shape[0]
        ranks = slot_ranks_by_expert(ids_ref[...], experts)
        spread = (iota((slots, experts), 0) // MAIN == iota((slots, experts), 1)).astype(F32)
        at = dot(spread.astype(BF16), ranks.astype(BF16))
        sub = iota((slots, tokens), 0) % MAIN
        main = (at == sub.astype(F32)).astype(F32).astype(BF16)
        last = at == float(MAIN)
        block = width // MAIN
        square = jnp.zeros((tokens, 1), F32)
        for part in range(MAIN):
            piece = h_ref[:, part * block : (part + 1) * block]
            square += jnp.sum(piece * piece, axis=1, keepdims=True)
        norm = 1.0 / jnp.sqrt(square / width + 1e-06)
        folded = jnp.zeros((slots, block), F32)
        for part in range(MAIN):
            here = slice(part * block, (part + 1) * block)
            normed = (h_ref[:, here] * norm * gain_ref[:, here]).astype(BF16)
            rows_ref[:, here] = dot(main, normed).astype(BF16)
            ninth = (last & (sub == part)).astype(F32).astype(BF16)
            folded += dot(ninth, normed)
        rows_ref[:, width:] = folded.astype(BF16)


def attend(place, queries, own_kv, far_kv, cos2, sin2, residual, gain, ids_t, experts):
    tokens, width = queries.shape
    cols = STEP_HEADS * HEAD_DIM
    steps = width // cols
    per_kv = steps // KV_HEADS
    near = own_kv.shape[0]
    block = width // MAIN
    whole = lambda shape: pl.BlockSpec(shape, lambda i, place: (0,) * len(shape))
    return pl.pallas_call(
        attend_kernel,
        grid_spec=pltpu.PrefetchScalarGridSpec(
            num_scalar_prefetch=1,
            grid=(steps,),
            in_specs=[
                pl.BlockSpec((tokens, cols), lambda i, place: (0, i)),
                pl.BlockSpec((near, HEAD_DIM), lambda i, place: (0, i // per_kv)),
                pl.BlockSpec((near, HEAD_DIM), lambda i, place: (0, KV_HEADS + i // per_kv)),
                pl.BlockSpec((near, HEAD_DIM), lambda i, place: (0, i // per_kv)),
                pl.BlockSpec((near, HEAD_DIM), lambda i, place: (0, KV_HEADS + i // per_kv)),
                whole((tokens, HEAD_DIM)),
                whole((tokens, HEAD_DIM)),
                pl.BlockSpec((tokens, cols), lambda i, place: (0, i)),
                whole((1, width)),
                whole((TOP, tokens)),
            ],
            out_specs=[
                whole((tokens, width)),
                whole((experts * MAIN, width + block)),
            ],
        ),
        out_shape=[
            jax.ShapeDtypeStruct((tokens, width), F32),
            jax.ShapeDtypeStruct((experts * MAIN, width + block), BF16),
        ],
        compiler_params=params(48),
        name="attend",
    )(place, queries, own_kv, own_kv, far_kv, far_kv, cos2, sin2, residual, gain, ids_t)


def gate_up_kernel(rows_ref, weights_ref, act_ref, x_ref):
    slots = rows_ref.shape[0]
    width = x_ref.shape[1]
    experts = slots // MAIN
    block = width // MAIN

    @pl.when(pl.program_id(0) == 0)
    def _():
        x_ref[:slots, :] = rows_ref[:, :width]
        folded = rows_ref[:, width:]
        row, col = iota((experts, slots), 0), iota((experts, slots), 1)
        for part in range(MAIN):
            pick = (col == row * MAIN + part).astype(F32).astype(BF16)
            x_ref[slots:, part * block : (part + 1) * block] = dot(pick, folded).astype(BF16)

    def silu(v):
        return v / (1.0 + jnp.exp(-v))

    tails = []
    for shard in range(2):
        both = dot(x_ref[...], weights_ref[shard])
        gate, upper, tail = both[:, :128], both[:, 128:256], both[:, 256:]
        act_ref[:, shard * 128 : (shard + 1) * 128] = (silu(gate) * upper).astype(BF16)
        tails.append(silu(tail) * pltpu.roll(tail, HALF, 1))
    lane = iota(tails[0].shape, 1)
    act_ref[:, 256:] = jnp.where(lane < HALF, tails[0], pltpu.roll(tails[1], HALF, 1)).astype(BF16)


def gate_up(rows, weights):
    slots, wide = rows.shape
    shards, width, cols = weights.shape
    total = slots + slots // MAIN
    return pl.pallas_call(
        gate_up_kernel,
        grid=(shards // 2,),
        in_specs=[
            pl.BlockSpec((slots, wide), lambda i: (0, 0)),
            pl.BlockSpec((2, width, cols), lambda i: (i, 0, 0)),
        ],
        out_specs=pl.BlockSpec((total, cols), lambda i: (0, i)),
        out_shape=jax.ShapeDtypeStruct((total, cols * shards // 2), BF16),
        scratch_shapes=[pltpu.VMEM((total, width), BF16)],
        compiler_params=params(48),
        cost_estimate=pl.CostEstimate(
            flops=2 * total * width * cols * shards,
            bytes_accessed=2 * weights.size + 4 * rows.size,
            transcendentals=0,
        ),
        name="gate_up",
    )(rows, weights)


def down_kernel(place_ref, own_a, own_b, far_a, far_b, weights_ref, out_ref, fold_ref):
    step = pl.program_id(0)
    slots = out_ref.shape[1]
    experts = slots // MAIN
    cols = weights_ref.shape[3]
    piece = fold_ref.shape[2]
    parts = cols // piece
    mine = place_ref[0]
    first = weights_ref[0, mine]
    second = weights_ref[0, 1 - mine]

    @pl.when(step == 0)
    def _():
        fold_ref[...] = jnp.zeros_like(fold_ref)

    for group, (a, b) in enumerate(((own_a, own_b), (far_a, far_b))):
        to = mine if group == 0 else 1 - mine
        y = (dot(a[...], first) + dot(b[...], second)).astype(BF16)
        start = pl.multiple_of(step * cols, 128)
        out_ref[to, :, pl.ds(start, cols)] = y[:slots]
        row, col = iota((slots, experts), 0), iota((slots, experts), 1)
        for part in range(parts):
            put = (row == col * MAIN + step * parts + part).astype(F32).astype(BF16)
            fold_ref[group] += dot(put, y[slots:, part * piece : (part + 1) * piece])

    @pl.when(step == pl.num_programs(0) - 1)
    def _():
        out_ref[mine, :, out_ref.shape[2] - piece :] = fold_ref[0].astype(BF16)
        out_ref[1 - mine, :, out_ref.shape[2] - piece :] = fold_ref[1].astype(BF16)


def down(place, own_a, own_b, far_a, far_b, weights):
    total, half = own_a.shape
    shards, _, _, cols = weights.shape
    slots = total * MAIN // (MAIN + 1)
    piece = shards * cols // MAIN
    acts = pl.BlockSpec((total, half), lambda i, place: (0, 0))
    return pl.pallas_call(
        down_kernel,
        grid_spec=pltpu.PrefetchScalarGridSpec(
            num_scalar_prefetch=1,
            grid=(shards,),
            in_specs=[acts] * 4
            + [pl.BlockSpec((1, 2, half, cols), lambda i, place: (i, 0, 0, 0))],
            out_specs=pl.BlockSpec((2, slots, shards * cols + piece), lambda i, place: (0, 0, 0)),
            scratch_shapes=[pltpu.VMEM((2, slots, piece), F32)],
        ),
        out_shape=jax.ShapeDtypeStruct((2, slots, shards * cols + piece), BF16),
        compiler_params=params(48),
        name="down",
    )(place, own_a, own_b, far_a, far_b, weights)


def combine_kernel(ids_ref, weights_ref, h_ref, back_ref, out_ref):
    tokens = h_ref.shape[0]
    slots = back_ref.shape[1]
    experts = slots // MAIN
    width = h_ref.shape[1]
    piece = width // MAIN
    expert = iota((tokens, experts), 1)
    named = jnp.zeros((tokens, experts), F32)
    weight = jnp.zeros((tokens, experts), F32)
    for choice in range(TOP):
        match = ids_ref[:, choice : choice + 1] == expert
        named += match.astype(F32)
        weight += jnp.where(match, weights_ref[:, choice : choice + 1], 0.0)
    earlier = (iota((tokens, tokens), 1) < iota((tokens, tokens), 0)).astype(F32)
    rank = jnp.where(named > 0.5, dot(earlier.astype(BF16), named.astype(BF16)), 255.0)
    spread = (iota((experts, slots), 1) // MAIN == iota((experts, slots), 0)).astype(F32)
    spread = spread.astype(BF16)
    at = dot(rank.astype(BF16), spread)
    sub = iota((tokens, slots), 1) % MAIN
    levels = []
    rest = weight
    for _ in range(3):
        level = rest.astype(BF16)
        rest = rest - level.astype(F32)
        levels.append(dot(level, spread))
    main = [jnp.where(at == sub.astype(F32), level, 0.0).astype(BF16) for level in levels]
    last = [jnp.where(at == float(MAIN), level, 0.0) for level in levels]
    main = jnp.concatenate(main, axis=0)

    def add_up(stacked):
        return stacked[:tokens] + (stacked[tokens : 2 * tokens] + stacked[2 * tokens :])

    for part in range(MAIN):
        here = slice(part * piece, (part + 1) * piece)
        ninth = jnp.concatenate(
            [jnp.where(sub == part, level, 0.0).astype(BF16) for level in last], axis=0
        )
        summed = dot(main, back_ref[0, :, here]) + dot(ninth, back_ref[0, :, width:])
        out_ref[:, here] = (h_ref[:, here] + add_up(summed)).astype(BF16)


def combine(ids, weights, h_state, back):
    tokens, width = h_state.shape
    halves, slots, wide = back.shape
    part = width // halves
    return pl.pallas_call(
        combine_kernel,
        grid=(halves,),
        in_specs=[
            pl.BlockSpec((tokens, TOP), lambda i: (0, 0)),
            pl.BlockSpec((tokens, TOP), lambda i: (0, 0)),
            pl.BlockSpec((tokens, part), lambda i: (0, i)),
            pl.BlockSpec((1, slots, wide), lambda i: (i, 0, 0)),
        ],
        out_specs=pl.BlockSpec((tokens, part), lambda i: (0, i)),
        out_shape=jax.ShapeDtypeStruct((tokens, width), BF16),
        compiler_params=params(48),
        name="combine",
    )(ids, weights, h_state, back)


def swap(x):
    return lax.ppermute(x, "y", [(0, 1), (1, 0)])


def per_device(
    queries,
    keys,
    values,
    positions,
    residual,
    norm_gain,
    expert_ids,
    route_weights,
    w_gate,
    w_up,
    w_down,
):
    width = queries.shape[2]
    owners = lax.axis_size("exp")
    place = jnp.stack([lax.axis_index("y"), lax.axis_index("x")]).astype(jnp.int32)

    cosine, sine = yarn_tables(positions[0])
    cos2 = jnp.concatenate([cosine, cosine], axis=1)
    sin2 = jnp.concatenate([-sine, sine], axis=1)
    kv = pack_kv(keys[0], values[0], cos2, sin2)
    own_kv = lax.all_gather(kv, "x", axis=0, tiled=True)
    far_kv = lax.ppermute(own_kv, "y", [(0, 1)])

    gate, upper = w_gate[0], w_up[0]
    both = jnp.concatenate(
        [gate[:, :128], upper[:, :128], gate[:, 128:], upper[:, 128:]], axis=1
    )
    both = lax.all_gather(both, "x", axis=0)
    hidden, cols = w_down.shape[1:]
    lower = w_down[0].reshape(4, 2, hidden // 8, cols)
    lower = jnp.concatenate(
        [lower[:, :, :128].reshape(4, 256, cols), lower[:, :, 128:].reshape(4, 128, cols)], axis=1
    )
    lower = lax.all_gather(lower.reshape(hidden, cols), "x", axis=0)
    lower = lower.reshape(lower.shape[0], 2, hidden // 2, cols)

    h_state, rows = attend(
        place, queries[0], own_kv, far_kv, cos2, sin2, residual[0], norm_gain[None],
        expert_ids[0].T, owners,
    )
    slots = owners * MAIN
    wide = rows.shape[1]
    arrived = lax.all_to_all(
        rows.reshape(owners, MAIN, wide), "exp", split_axis=0, concat_axis=0, tiled=True
    ).reshape(slots, wide)
    passed = swap(arrived)
    own_a = gate_up(arrived, both)
    far_b = swap(own_a)
    far_a = gate_up(passed, both)
    own_b = swap(far_a)
    out = down(place, own_a, own_b, far_a, far_b, lower)
    back = lax.all_to_all(
        out.reshape(2 * owners, MAIN, out.shape[2]),
        ("y", "exp"),
        split_axis=0,
        concat_axis=0,
        tiled=True,
    ).reshape(out.shape)
    return combine(expert_ids[0], route_weights[0], h_state, back)[None]


def solution(mesh):
    inner = Mesh(mesh.devices.reshape(2, 4, mesh.shape["exp"]), ("y", "x", "exp"))
    ctx = ("y", "x")
    return jax.shard_map(
        per_device,
        mesh=inner,
        in_specs=(
            P("exp", ctx, None),
            P("exp", ctx, None),
            P("exp", ctx, None),
            P("exp", ctx),
            P("exp", ctx, None),
            P(),
            P("exp", ctx, None),
            P("exp", ctx, None),
            P("exp", None, ctx),
            P("exp", None, ctx),
            P("exp", None, ctx),
        ),
        out_specs=P("exp", ctx, None),
        check_vma=False,
    )
```

time: 676 us -> 297 us (0.44)
  waiting for transfers between devices: 381 us -> 101 us
  blocking collectives: 142 us -> 83 us
  matrix products: 51.7 us -> 0 us
  Pallas kernels: 0 us -> 49.8 us
  other arithmetic: 26.6 us -> 4.28 us
  local copies, waits for them, and re-layouts: 46 us -> 25.7 us
  starting transfers between devices: 11.8 us -> 18.6 us
    all_gather x3 -> x2, waiting for transfers between devices: 288 us -> 14.9 us  [the longest x1 11.8 us: per_device(): lower = lax.all_gather(lower.reshape(hidden, cols), 'x', axis=0)]
    all_to_all x2 -> x1, blocking collectives: 142 us -> 71.3 us  [per_device(): lax.all_to_all(rows.reshape(owners, MAIN, wide), 'exp', split_axis=0, con...]
    dot_general x7 -> x0, matrix products: 51.7 us -> none  [the longest x1 12.6 us: per_device(): gate = jnp.dot(hidden_piece, gate_local, preferred_element_type=jnp.float32)]
    pallas_call x0 -> x6, Pallas kernels: none -> 49.8 us  [the longest x2 19 us: gate_up(): pl.pallas_call(gate_up_kernel, grid=(shards // 2,), in_specs=[pl.BlockSpe...]
    all_to_all x1, waiting for transfers between devices: 93.8 us -> 56.4 us  [per_device(): lax.all_to_all(out.reshape(2 * owners, MAIN, out.shape[2]), ('y', 'exp'),...]
    ppermute x0 -> x4, waiting for transfers between devices: none -> 29.9 us  [the longest x3 21.1 us: swap(): return lax.ppermute(x, 'y', [(0, 1), (1, 0)])]
    reshape x5 -> x0, local copies, waits for them, and re-layouts: 23 us -> none  [the longest x2 9.03 us: per_device(): out_cols = out_cols.reshape(ctx_count, owners, capacity, out_cols.shape[1])]
    all_gather x0 -> x1, local copies, waits for them, and re-layouts: none -> 16.7 us  [per_device(): both = lax.all_gather(both, 'x', axis=0)]
  transfers between devices with their start and end apart: 4 -> 7, of which waited for: 4 -> 5; matrix products, arithmetic and copies ran while one was open for 3% -> 7% of each run, Pallas kernels for 0% -> 13%
where the time goes in v1:
time: 297 us; the launch traced here: 296 us
  waiting for transfers between devices  101 us (34%)
  blocking collectives  83 us (28%)
  Pallas kernels  49.8 us (17%)
  local copies, waits for them, and re-layouts  25.7 us (9%)
  starting transfers between devices  18.6 us (6%)
  between operations  13.6 us (5%)
  other arithmetic  4.28 us (1%)
    all_to_all x1, blocking collectives, per_device(): lax.all_to_all(rows.reshape(owners, MAIN, wide), 'exp', split_axis=0, con...  71.3 us
    all_to_all x1, waiting for transfers between devices, per_device(): lax.all_to_all(out.reshape(2 * owners, MAIN, out.shape[2]), ('y', 'exp'),...  56.4 us
    ppermute x3, waiting for transfers between devices, swap(): return lax.ppermute(x, 'y', [(0, 1), (1, 0)])  21.1 us
    pallas_call x2, Pallas kernels, gate_up(): pl.pallas_call(gate_up_kernel, grid=(shards // 2,), in_specs=[pl.BlockSpe...  19 us
    all_gather x1, local copies, waits for them, and re-layouts, per_device(): both = lax.all_gather(both, 'x', axis=0)  16.7 us
    pallas_call x1, Pallas kernels, attend(): pl.pallas_call(attend_kernel, grid_spec=pltpu.PrefetchScalarGridSpec(num_...  16.6 us
    all_gather x1, waiting for transfers between devices, per_device(): lower = lax.all_gather(lower.reshape(hidden, cols), 'x', axis=0)  11.8 us
    all_gather x1, blocking collectives, per_device(): own_kv = lax.all_gather(kv, 'x', axis=0, tiled=True)  11.7 us
  transfers between devices with their start and end apart: 7, of which 5 were waited for; matrix products, arithmetic and copies ran while one was open for 7% of the time, Pallas kernels for 13%

profile of v1, /device:TPU:17, one launch (start us, length us, event | category | flops | bytes accessed | tf_op | source)
XLA Modules:
  0.0 296.3 jit_solution(16387740550377818439)
XLA Ops:
  6.5 0.0 all-gather.6.cloned.1.call-start
  6.5 1.2 slice.26
  7.7 1.3 slice.24
  9.1 0.1 slice.25
  9.2 1.8 pad_maximum_fusion
  11.0 0.0 all-gather.6.cloned.1.call-update
  11.0 0.0 all-gather.4.cloned.1.call-start
  11.1 1.3 copy-done.10
  12.5 0.0 copy-start.12
  12.5 0.1 slice.28
  12.6 0.0 copy-start.3
  12.6 0.0 copy-start.4
  12.6 0.0 copy-start.7
  12.6 0.0 copy-start.8
  12.7 1.3 pad_maximum_fusion.1
  13.9 0.0 all-gather.4.cloned.1.call-update
  14.0 0.3 fusion.2
  14.3 0.7 pad_maximum_fusion.2
  15.1 1.7 pack_kv.1
  16.8 11.7 %all_gather.12.own_k_ref.own_v_ref = bf16[512,512]{1,0:T(8,128)(2,1)S(1)} all-gather(bf16[128,512]{1,0:T(8,128)(2,1)} %pack_kv.1), channel_id=1, replica_groups=mesh['y'=2,'x'=4,'exp'=32] {'x'}, dimensions={0}, use_global_device_ids=true | all-gather | bytes 655360 | tf_op jit(solution)/shard_map/all_gather | solution.py:382
  28.5 2.9 collective-permute-start
  31.4 0.1 pad_add_fusion.place_ref
  31.5 8.8 %collective-permute-done.far_k_ref.far_v_ref = bf16[512,512]{1,0:T(8,128)(2,1)S(1)} collective-permute-done((bf16[512,512]{1,0:T(8,128)(2,1)S(1)}, bf16[512,512]{1,0:T(8,128)(2,1)S(1)}, u32[]{:S(2)}, u32[]{:S(2)}) %collective-permute-start) | collective-permute-done | bytes 524320 | tf_op jit(solution)/shard_map/ppermute | solution.py:383
  40.2 0.0 copy-done.3
  40.3 0.0 copy-start.5
  40.3 0.8 copy-done.5
  41.1 0.8 copy-done.6
  41.9 16.6 %attend.1 = (f32[128,4096]{1,0:T(8,128)S(1)}, bf16[256,4608]{1,0:T(8,128)(2,1)}) custom-call(s32[2]{0:T(128)S(1)} %pad_add_fusion.place_ref, bf16[128,4096]{1,0:T(8,128)(2,1)S(1)} %bitcast.30, bf16[512,512]{1,0:T(8,128)(2,1)S(1)} %all_gather.12.own_k_ref.own_v_ref, bf16[512,512]{1,0:T(8,128)(2,1)S(1)} %all_gather.12.own_k_ref.own_v_ref, ...), custom_call_target="tpu_custom_call" | custom-call | tf_op jit(solution)/shard_map/attend/pallas_call | solution.py:160
  58.5 71.3 %all_to_all.10 = bf16[32,8,4608]{2,1,0:T(8,128)(2,1)S(1)} all-to-all(bf16[32,8,4608]{2,1,0:T(8,128)(2,1)} %bitcast.41), channel_id=1, replica_groups=mesh['y'=2,'x'=4,'exp'=32] {'exp'}, dimensions={0} | all-to-all | bytes 4718592 | tf_op jit(solution)/shard_map/all_to_all | solution.py:404
  129.8 2.2 collective-permute-start.1
  132.0 3.1 %all-gather.6.cloned.1.call-done = bf16[16384,384]{0,1:T(8,128)(2,1)} async-done(((bf16[4096,384]{0,1:T(8,128)(2,1)}), bf16[16384,384]{0,1:T(8,128)(2,1)}) %all-gather.6.cloned.1.call-update) | async-done | bytes 12582928 | tf_op jit(solution)/shard_map/all_gather | solution.py:389
  135.1 16.7 %copy.19 = bf16[16384,384]{1,0:T(8,128)(2,1)} copy(bf16[16384,384]{0,1:T(8,128)(2,1)} %all-gather.6.cloned.1.call-done) | data formatting | bytes 25165824 | tf_op jit(solution)/shard_map/all_gather | solution.py:389
  151.8 9.4 %gate_up.2.own_a = bf16[288,768]{1,0:T(8,128)(2,1)S(1)} custom-call(bf16[256,4608]{1,0:T(8,128)(2,1)S(1)} %bitcast.27, bf16[4,4096,384]{2,1,0:T(8,128)(2,1)} %bitcast.36), custom_call_target="tpu_custom_call" | custom-call | flops 3623878656 | bytes 17301504 | tf_op jit(solution)/shard_map/gate_up/pallas_call | solution.py:223
  161.1 1.0 collective-permute-start.3
  162.1 21.1 %collective-permute-done.1.rows_ref = bf16[256,4608]{1,0:T(8,128)(2,1)} collective-permute-done((bf16[256,4608]{1,0:T(8,128)(2,1)S(1)}, bf16[256,4608]{1,0:T(8,128)(2,1)}, u32[]{:S(2)}, u32[]{:S(2)}) %collective-permute-start.1) | collective-permute-done | bytes 2359328 | tf_op jit(solution)/shard_map/ppermute | solution.py:358
  183.3 9.7 %gate_up.3.far_a = bf16[288,768]{1,0:T(8,128)(2,1)S(1)} custom-call(bf16[256,4608]{1,0:T(8,128)(2,1)} %collective-permute-done.1.rows_ref, bf16[4,4096,384]{2,1,0:T(8,128)(2,1)} %bitcast.37), custom_call_target="tpu_custom_call" | custom-call | flops 3623878656 | bytes 17301504 | tf_op jit(solution)/shard_map/gate_up/pallas_call | solution.py:223
  192.9 1.4 collective-permute-start.2
  194.4 11.8 %all-gather.4.cloned.1.call-done = bf16[4,1536,512]{2,1,0:T(8,128)(2,1)} async-done(((bf16[1,1536,512]{2,1,0:T(8,128)(2,1)}), bf16[4,1536,512]{2,1,0:T(8,128)(2,1)}) %all-gather.4.cloned.1.call-update) | async-done | bytes 6291472 | tf_op jit(solution)/shard_map/all_gather | solution.py:395
  206.2 0.0 collective-permute-done.3.far_b
  206.2 0.0 collective-permute-done.2.own_b
  206.2 8.5 %down.1 = bf16[2,256,2304]{2,1,0:T(8,128)(2,1)S(1)} custom-call(s32[2]{0:T(128)S(1)} %pad_add_fusion.place_ref, bf16[288,768]{1,0:T(8,128)(2,1)S(1)} %gate_up.2.own_a, bf16[288,768]{1,0:T(8,128)(2,1)S(1)} %collective-permute-done.2.own_b, bf16[288,768]{1,0:T(8,128)(2,1)S(1)} %gate_up.3.far_a, bf16[288,768]{1,0:T(8,128)(2,1)S(1)} %collective-permute-done.3.far_b, ...), custom_call_target="tpu_custom_call" | custom-call | tf_op jit(solution)/shard_map/down/pallas_call | solution.py:280
  214.8 1.4 copy-done
  216.2 11.0 %all-to-all-start.1 = ((bf16[64,8,2304]{2,1,0:T(8,128)(2,1)}), bf16[64,8,2304]{2,1,0:T(8,128)(2,1)S(1)}, u32[]{:S(2)}, u32[]{:S(2)}) async-start(bf16[64,8,2304]{2,1,0:T(8,128)(2,1)} %bitcast.29), calls=%async_computation.1 | async-start | bytes 4718592 | tf_op jit(solution)/shard_map/all_to_all | solution.py:413
  227.2 0.1 copy.16
  227.3 0.1 copy.17
  227.4 56.4 %all-to-all-done.1 = bf16[64,8,2304]{2,1,0:T(8,128)(2,1)S(1)} async-done(((bf16[64,8,2304]{2,1,0:T(8,128)(2,1)}), bf16[64,8,2304]{2,1,0:T(8,128)(2,1)S(1)}, u32[]{:S(2)}, u32[]{:S(2)}) %all-to-all-start.1) | async-done | bytes 2359328 | tf_op jit(solution)/shard_map/all_to_all | solution.py:413
  283.8 1.6 copy-done.2
  285.4 4.0 %combine.1 = bf16[128,4096]{1,0:T(8,128)(2,1)} custom-call(s32[128,8]{1,0:T(8,128)S(1)} %bitcast.32, f32[128,8]{1,0:T(8,128)S(1)} %bitcast.33, f32[128,4096]{1,0:T(8,128)S(1)} %copy-done.2, bf16[2,256,2304]{2,1,0:T(8,128)(2,1)S(1)} %bitcast.28), custom_call_target="tpu_custom_call" | custom-call | tf_op jit(solution)/shard_map/combine/pallas_call | solution.py:341
  (18 shorter events, 0.1 us)
Async XLA Ops:
  6.5 2.5 copy-start.9
  6.5 128.6 %all-gather.6.cloned.1.call-start = ((), (), s32[]{:S(2)}) async-start(), calls=%async_computation.3 | async-start | bytes 15728640 | tf_op jit(solution)/shard_map/all_gather | solution.py:389
  11.0 1.4 copy-start.10
  11.0 195.2 %all-gather.4.cloned.1.call-start = ((), (), s32[]{:S(2)}) async-start(), calls=%async_computation.2 | async-start | bytes 7864320 | tf_op jit(solution)/shard_map/all_gather | solution.py:395
  12.5 1.5 copy-start.12
  12.6 27.6 %copy-start.3 = (bf16[1,128,4096]{2,1,0:T(8,128)(2,1)S(1)}, bf16[1,128,4096]{2,1,0:T(8,128)(2,1)}, u32[]{:S(2)}) copy-start(bf16[1,128,4096]{2,1,0:T(8,128)(2,1)} %param.11) | copy-start | bytes 3145732
  12.6 27.6 %copy-start.4 = (bf16[1,128,4096]{2,1,0:T(8,128)(2,1)S(1)}, bf16[1,128,4096]{2,1,0:T(8,128)(2,1)}, u32[]{:S(2)}) copy-start(bf16[1,128,4096]{2,1,0:T(8,128)(2,1)} %param.15) | copy-start | bytes 3145732
  12.6 27.6 %copy-start.7 = (f32[4096]{0:T(1024)S(1)}, f32[4096]{0:T(1024)}, u32[]{:S(2)}) copy-start(f32[4096]{0:T(1024)} %param.16) | copy-start | bytes 49156
  12.6 27.6 %copy-start.8 = (s32[1,128,8]{1,2,0:T(8,128)S(1)}, s32[1,128,8]{1,2,0:T(8,128)}, u32[]{:S(2)}) copy-start(s32[1,128,8]{1,2,0:T(8,128)} %param.17) | copy-start | bytes 12292
  28.5 11.8 %collective-permute-start = (bf16[512,512]{1,0:T(8,128)(2,1)S(1)}, bf16[512,512]{1,0:T(8,128)(2,1)S(1)}, u32[]{:S(2)}, u32[]{:S(2)}) collective-permute-start(bf16[512,512]{1,0:T(8,128)(2,1)S(1)} %all_gather.12.own_k_ref.own_v_ref), channel_id=1, source_target_pairs={{0,128},{1,129},{2,130},{3,131},{4,132},{5,133},{6,134},{7,135},{8... | collective-permute-start | bytes 1572872 | tf_op jit(solution)/shard_map/ppermute | solution.py:383
  40.3 0.8 copy-start.5
  41.1 0.8 copy-start.6
  58.5 71.3 %copy-start.1 = (f32[128,4096]{1,0:T(8,128)}, f32[128,4096]{1,0:T(8,128)S(1)}, u32[]{:S(2)}) copy-start(f32[128,4096]{1,0:T(8,128)S(1)} %get-tuple-element.7.h_ref) | copy-start | bytes 6291460
  129.8 53.4 %collective-permute-start.1 = (bf16[256,4608]{1,0:T(8,128)(2,1)S(1)}, bf16[256,4608]{1,0:T(8,128)(2,1)}, u32[]{:S(2)}, u32[]{:S(2)}) collective-permute-start(bf16[256,4608]{1,0:T(8,128)(2,1)S(1)} %bitcast.26), channel_id=1, source_target_pairs={{0,128},{128,0},{1,129},{129,1},{2,130},{130,2},{3,131},{131,3},{4... | collective-permute-start | bytes 7077896 | tf_op jit(solution)/shard_map/ppermute | solution.py:358
  161.1 45.1 %collective-permute-start.3 = (bf16[288,768]{1,0:T(8,128)(2,1)S(1)}, bf16[288,768]{1,0:T(8,128)(2,1)S(1)}, u32[]{:S(2)}, u32[]{:S(2)}) collective-permute-start(bf16[288,768]{1,0:T(8,128)(2,1)S(1)} %gate_up.2.own_a), channel_id=1, source_target_pairs={{0,128},{128,0},{1,129},{129,1},{2,130},{130,2},{3,131},{131,3},{4... | collective-permute-start | bytes 1327112 | tf_op jit(solution)/shard_map/ppermute | solution.py:358
  192.9 13.3 %collective-permute-start.2 = (bf16[288,768]{1,0:T(8,128)(2,1)S(1)}, bf16[288,768]{1,0:T(8,128)(2,1)S(1)}, u32[]{:S(2)}, u32[]{:S(2)}) collective-permute-start(bf16[288,768]{1,0:T(8,128)(2,1)S(1)} %gate_up.3.far_a), channel_id=1, source_target_pairs={{0,128},{128,0},{1,129},{129,1},{2,130},{130,2},{3,131},{131,3},{4... | collective-permute-start | bytes 1327112 | tf_op jit(solution)/shard_map/ppermute | solution.py:358
  214.7 1.4 copy-start
  216.2 11.1 %copy-start.11 = (f32[1,128,8]{1,2,0:T(8,128)S(1)}, f32[1,128,8]{1,2,0:T(8,128)}, u32[]{:S(2)}) copy-start(f32[1,128,8]{1,2,0:T(8,128)} %param.18) | copy-start | bytes 12292
  216.2 67.6 %all-to-all-start.1 = ((bf16[64,8,2304]{2,1,0:T(8,128)(2,1)}), bf16[64,8,2304]{2,1,0:T(8,128)(2,1)S(1)}, u32[]{:S(2)}, u32[]{:S(2)}) async-start(bf16[64,8,2304]{2,1,0:T(8,128)(2,1)} %bitcast.29), calls=%async_computation.1 | async-start | bytes 4718592 | tf_op jit(solution)/shard_map/all_to_all | solution.py:413
  283.8 1.6 copy-start.2
Sparse Core Ops, SparseCore 0:
  11.2 123.8 all-gather.5
  136.9 69.2 all-gather.3

commit v2 on v1

--- a/solution.py
+++ b/solution.py
@@ -15,6 +15,7 @@
 TOP = 8
 HALF = HEAD_DIM // 2
 STEP_HEADS = 4
+FIRST = 5
 MAIN = 8
 
 F32 = jnp.float32
@@ -75,6 +76,26 @@
     )(keys, values, cos2, sin2)
 
 
+def pack_weights_kernel(gate_ref, upper_ref, out_ref):
+    both = jnp.concatenate(
+        [gate_ref[:128], upper_ref[:128], gate_ref[128:], upper_ref[128:]], axis=0
+    )
+    out_ref[...] = both.T
+
+
+def pack_weights(gate, upper):
+    units, width = gate.shape
+    block = width // 4
+    return pl.pallas_call(
+        pack_weights_kernel,
+        grid=(width // block,),
+        in_specs=[pl.BlockSpec((units, block), lambda i: (0, i))] * 2,
+        out_specs=pl.BlockSpec((block, 2 * units), lambda i: (i, 0)),
+        out_shape=jax.ShapeDtypeStruct((width, 2 * units), BF16),
+        name="pack_weights",
+    )(gate, upper)
+
+
 def slot_ranks_by_expert(ids_t, experts):
     tokens = ids_t.shape[1]
     expert = iota((experts, tokens), 0)
@@ -88,7 +109,7 @@
 
 def attend_kernel(
     place_ref, q_ref, own_k_ref, own_v_ref, far_k_ref, far_v_ref, cos_ref, sin_ref, residual_ref,
-    gain_ref, ids_ref, h_ref, rows_ref,
+    gain_ref, ids_ref, h_ref, one_ref, two_ref,
 ):
     step = pl.program_id(0)
     tokens = q_ref.shape[0]
@@ -125,8 +146,8 @@
 
     @pl.when(step == pl.num_programs(0) - 1)
     def _():
-        experts = rows_ref.shape[0] // MAIN
-        slots = rows_ref.shape[0]
+        slots, first = one_ref.shape
+        experts = slots // MAIN
         ranks = slot_ranks_by_expert(ids_ref[...], experts)
         spread = (iota((slots, experts), 0) // MAIN == iota((slots, experts), 1)).astype(F32)
         at = dot(spread.astype(BF16), ranks.astype(BF16))
@@ -143,10 +164,14 @@
         for part in range(MAIN):
             here = slice(part * block, (part + 1) * block)
             normed = (h_ref[:, here] * norm * gain_ref[:, here]).astype(BF16)
-            rows_ref[:, here] = dot(main, normed).astype(BF16)
+            sent = dot(main, normed).astype(BF16)
+            if (part + 1) * block <= first:
+                one_ref[:, here] = sent
+            else:
+                two_ref[:, part * block - first : (part + 1) * block - first] = sent
             ninth = (last & (sub == part)).astype(F32).astype(BF16)
             folded += dot(ninth, normed)
-        rows_ref[:, width:] = folded.astype(BF16)
+        two_ref[:, width - first :] = folded.astype(BF16)
 
 
 def attend(place, queries, own_kv, far_kv, cos2, sin2, residual, gain, ids_t, experts):
@@ -156,6 +181,7 @@
     per_kv = steps // KV_HEADS
     near = own_kv.shape[0]
     block = width // MAIN
+    first = FIRST * block
     whole = lambda shape: pl.BlockSpec(shape, lambda i, place: (0,) * len(shape))
     return pl.pallas_call(
         attend_kernel,
@@ -176,121 +202,163 @@
             ],
             out_specs=[
                 whole((tokens, width)),
-                whole((experts * MAIN, width + block)),
+                whole((experts * MAIN, first)),
+                whole((experts * MAIN, width + block - first)),
             ],
         ),
         out_shape=[
             jax.ShapeDtypeStruct((tokens, width), F32),
-            jax.ShapeDtypeStruct((experts * MAIN, width + block), BF16),
+            jax.ShapeDtypeStruct((experts * MAIN, first), BF16),
+            jax.ShapeDtypeStruct((experts * MAIN, width + block - first), BF16),
         ],
         compiler_params=params(48),
         name="attend",
     )(place, queries, own_kv, own_kv, far_kv, far_kv, cos2, sin2, residual, gain, ids_t)
 
 
-def gate_up_kernel(rows_ref, weights_ref, act_ref, x_ref):
-    slots = rows_ref.shape[0]
+def gate_up_kernel(one_ref, two_ref, weights_ref, act_ref, x_ref, tail_ref):
+    slots, first = one_ref.shape
     width = x_ref.shape[1]
     experts = slots // MAIN
     block = width // MAIN
-
-    @pl.when(pl.program_id(0) == 0)
+    step = pl.program_id(0)
+
+    @pl.when(step == 0)
     def _():
-        x_ref[:slots, :] = rows_ref[:, :width]
-        folded = rows_ref[:, width:]
+        x_ref[:slots, :first] = one_ref[...]
+        x_ref[:slots, first:] = two_ref[:, : width - first]
+        folded = two_ref[:, width - first :]
         row, col = iota((experts, slots), 0), iota((experts, slots), 1)
         for part in range(MAIN):
             pick = (col == row * MAIN + part).astype(F32).astype(BF16)
             x_ref[slots:, part * block : (part + 1) * block] = dot(pick, folded).astype(BF16)
 
-    def silu(v):
-        return v / (1.0 + jnp.exp(-v))
-
-    tails = []
-    for shard in range(2):
-        both = dot(x_ref[...], weights_ref[shard])
-        gate, upper, tail = both[:, :128], both[:, 128:256], both[:, 256:]
-        act_ref[:, shard * 128 : (shard + 1) * 128] = (silu(gate) * upper).astype(BF16)
-        tails.append(silu(tail) * pltpu.roll(tail, HALF, 1))
-    lane = iota(tails[0].shape, 1)
-    act_ref[:, 256:] = jnp.where(lane < HALF, tails[0], pltpu.roll(tails[1], HALF, 1)).astype(BF16)
-
-
-def gate_up(rows, weights):
-    slots, wide = rows.shape
+    both = dot(x_ref[...], weights_ref[0])
+    gated = (silu(both[:, :128]) * both[:, 128:256]).astype(BF16)
+    tail = silu(both[:, 256:]) * pltpu.roll(both[:, 256:], HALF, 1)
+
+    @pl.when(step % 2 == 0)
+    def _():
+        act_ref[:, :128] = gated
+        tail_ref[...] = tail
+
+    @pl.when(step % 2 == 1)
+    def _():
+        act_ref[:, 128:256] = gated
+        lane = iota(tail.shape, 1)
+        act_ref[:, 256:] = jnp.where(lane < HALF, tail_ref[...], pltpu.roll(tail, HALF, 1)).astype(
+            BF16
+        )
+
+
+def silu(v):
+    return v / (1.0 + jnp.exp(-v))
+
+
+def gate_up(one, two, weights):
+    slots = one.shape[0]
     shards, width, cols = weights.shape
     total = slots + slots // MAIN
     return pl.pallas_call(
         gate_up_kernel,
-        grid=(shards // 2,),
+        grid=(shards,),
         in_specs=[
-            pl.BlockSpec((slots, wide), lambda i: (0, 0)),
-            pl.BlockSpec((2, width, cols), lambda i: (i, 0, 0)),
+            pl.BlockSpec(one.shape, lambda i: (0, 0)),
+            pl.BlockSpec(two.shape, lambda i: (0, 0)),
+            pl.BlockSpec((1, width, cols), lambda i: (i, 0, 0)),
         ],
-        out_specs=pl.BlockSpec((total, cols), lambda i: (0, i)),
+        out_specs=pl.BlockSpec((total, cols), lambda i: (0, i // 2)),
         out_shape=jax.ShapeDtypeStruct((total, cols * shards // 2), BF16),
-        scratch_shapes=[pltpu.VMEM((total, width), BF16)],
-        compiler_params=params(48),
+        scratch_shapes=[pltpu.VMEM((total, width), BF16), pltpu.VMEM((total, 128), F32)],
+        compiler_params=params(32),
         cost_estimate=pl.CostEstimate(
             flops=2 * total * width * cols * shards,
-            bytes_accessed=2 * weights.size + 4 * rows.size,
+            bytes_accessed=2 * weights.size + 2 * (one.size + two.size),
             transcendentals=0,
         ),
         name="gate_up",
-    )(rows, weights)
-
-
-def down_kernel(place_ref, own_a, own_b, far_a, far_b, weights_ref, out_ref, fold_ref):
+    )(one, two, weights)
+
+
+def down_kernel(
+    place_ref, own_a, own_b, far_a, far_b, *refs,
+):
+    weights, (out_ref, act_ref, fold_ref) = refs[:-3], refs[-3:]
     step = pl.program_id(0)
     slots = out_ref.shape[1]
     experts = slots // MAIN
-    cols = weights_ref.shape[3]
+    total = slots + experts
+    cols = weights[0].shape[1]
     piece = fold_ref.shape[2]
-    parts = cols // piece
-    mine = place_ref[0]
-    first = weights_ref[0, mine]
-    second = weights_ref[0, 1 - mine]
+    shards = (out_ref.shape[2] - piece) // cols
 
     @pl.when(step == 0)
     def _():
+        row = iota((total, 1), 0)
+        block = jnp.where(row < slots, row // MAIN, row - slots)
+        mine = (block // 2) % 2 == place_ref[2]
+        for half, own, far in ((place_ref[0], own_a, far_a), (1 - place_ref[0], own_b, far_b)):
+            near, away = own[...].astype(F32), far[...].astype(F32)
+            act_ref[half, :total] = jnp.where(mine, near, away).astype(BF16)
+            act_ref[half, total:] = jnp.where(mine, away, near).astype(BF16)
         fold_ref[...] = jnp.zeros_like(fold_ref)
 
-    for group, (a, b) in enumerate(((own_a, own_b), (far_a, far_b))):
-        to = mine if group == 0 else 1 - mine
-        y = (dot(a[...], first) + dot(b[...], second)).astype(BF16)
-        start = pl.multiple_of(step * cols, 128)
-        out_ref[to, :, pl.ds(start, cols)] = y[:slots]
+    def in_order(weights):
+        rows = []
+        for base in range(0, weights.shape[0], 384):
+            for start, size in ((0, 128), (192, 128), (128, 64), (320, 64)):
+                rows.append(weights[base + start : base + start + size])
+        return jnp.concatenate(rows, axis=0)
+
+    def multiply(top, bottom, shard):
+        y = dot(act_ref[0], in_order(top)) + dot(act_ref[1], in_order(bottom))
+        y = y.astype(BF16)
+        start = pl.multiple_of(shard * cols, 128)
         row, col = iota((slots, experts), 0), iota((slots, experts), 1)
-        for part in range(parts):
-            put = (row == col * MAIN + step * parts + part).astype(F32).astype(BF16)
-            fold_ref[group] += dot(put, y[slots:, part * piece : (part + 1) * piece])
-
-    @pl.when(step == pl.num_programs(0) - 1)
+        for to in range(2):
+            out_ref[to, :, pl.ds(start, cols)] = y[to * total : to * total + slots]
+            ninth = y[to * total + slots : (to + 1) * total]
+            for part in range(cols // piece):
+                at = shard * (cols // piece) + part
+                put = (row == col * MAIN + at).astype(F32).astype(BF16)
+                fold_ref[to] += dot(put, ninth[:, part * piece : (part + 1) * piece])
+
+    for number, ahead in enumerate((0, shards - 1, 1, 2)):
+
+        @pl.when(step == number)
+        def _(number=number, ahead=ahead):
+            top, bottom = weights[2 * number : 2 * number + 2]
+            multiply(top[...], bottom[...], (place_ref[1] + ahead) % shards)
+
+    @pl.when(step == shards - 1)
     def _():
-        out_ref[mine, :, out_ref.shape[2] - piece :] = fold_ref[0].astype(BF16)
-        out_ref[1 - mine, :, out_ref.shape[2] - piece :] = fold_ref[1].astype(BF16)
-
-
-def down(place, own_a, own_b, far_a, far_b, weights):
-    total, half = own_a.shape
-    shards, _, _, cols = weights.shape
+        for to in range(2):
+            out_ref[to, :, out_ref.shape[2] - piece :] = fold_ref[to].astype(BF16)
+
+
+def down(place, acts, weights):
+    total, half = acts[0].shape
+    cols = weights[0].shape[1]
+    shards = len(weights) // 2
     slots = total * MAIN // (MAIN + 1)
     piece = shards * cols // MAIN
-    acts = pl.BlockSpec((total, half), lambda i, place: (0, 0))
+    whole = lambda shape: pl.BlockSpec(shape, lambda i, place: (0,) * len(shape))
     return pl.pallas_call(
         down_kernel,
         grid_spec=pltpu.PrefetchScalarGridSpec(
             num_scalar_prefetch=1,
             grid=(shards,),
-            in_specs=[acts] * 4
-            + [pl.BlockSpec((1, 2, half, cols), lambda i, place: (i, 0, 0, 0))],
-            out_specs=pl.BlockSpec((2, slots, shards * cols + piece), lambda i, place: (0, 0, 0)),
-            scratch_shapes=[pltpu.VMEM((2, slots, piece), F32)],
+            in_specs=[whole(a.shape) for a in (*acts, *weights)],
+            out_specs=whole((2, slots, shards * cols + piece)),
+            scratch_shapes=[
+                pltpu.VMEM((2, 2 * total, half), BF16),
+                pltpu.VMEM((2, slots, piece), F32),
+            ],
         ),
         out_shape=jax.ShapeDtypeStruct((2, slots, shards * cols + piece), BF16),
-        compiler_params=params(48),
+        compiler_params=params(36),
         name="down",
-    )(place, own_a, own_b, far_a, far_b, weights)
+    )(place, *acts, *weights)
 
 
 def combine_kernel(ids_ref, weights_ref, h_ref, back_ref, out_ref):
@@ -358,6 +426,10 @@
     return lax.ppermute(x, "y", [(0, 1), (1, 0)])
 
 
+def ring(x, ahead):
+    return lax.ppermute(x, "x", [(i, (i + ahead) % 4) for i in range(4)])
+
+
 def per_device(
     queries,
     keys,
@@ -373,7 +445,9 @@
 ):
     width = queries.shape[2]
     owners = lax.axis_size("exp")
-    place = jnp.stack([lax.axis_index("y"), lax.axis_index("x")]).astype(jnp.int32)
+    y_high = (lax.axis_index("exp") >> 1) & 1
+    place = jnp.stack([lax.axis_index("y"), lax.axis_index("x"), lax.axis_index("y") ^ y_high])
+    place = place.astype(jnp.int32)
 
     cosine, sine = yarn_tables(positions[0])
     cos2 = jnp.concatenate([cosine, cosine], axis=1)
@@ -382,34 +456,49 @@
     own_kv = lax.all_gather(kv, "x", axis=0, tiled=True)
     far_kv = lax.ppermute(own_kv, "y", [(0, 1)])
 
-    gate, upper = w_gate[0], w_up[0]
-    both = jnp.concatenate(
-        [gate[:, :128], upper[:, :128], gate[:, 128:], upper[:, 128:]], axis=1
-    )
-    both = lax.all_gather(both, "x", axis=0)
+    both = pack_weights(w_gate[0].T, w_up[0].T)
+    both = lax.all_gather(both, "x", axis=0, tiled=True).reshape(4, width, both.shape[1])
     hidden, cols = w_down.shape[1:]
-    lower = w_down[0].reshape(4, 2, hidden // 8, cols)
-    lower = jnp.concatenate(
-        [lower[:, :, :128].reshape(4, 256, cols), lower[:, :, 128:].reshape(4, 128, cols)], axis=1
-    )
-    lower = lax.all_gather(lower.reshape(hidden, cols), "x", axis=0)
-    lower = lower.reshape(lower.shape[0], 2, hidden // 2, cols)
-
-    h_state, rows = attend(
+    here = (w_down[0, : hidden // 2], w_down[0, hidden // 2 :])
+    left_top, right_bottom = ring(here[0], 1), ring(here[1], -1)
+    left_bottom, right_top = ring(here[1], 1), ring(here[0], -1)
+
+    h_state, one, two = attend(
         place, queries[0], own_kv, far_kv, cos2, sin2, residual[0], norm_gain[None],
         expert_ids[0].T, owners,
     )
-    slots = owners * MAIN
-    wide = rows.shape[1]
-    arrived = lax.all_to_all(
-        rows.reshape(owners, MAIN, wide), "exp", split_axis=0, concat_axis=0, tiled=True
-    ).reshape(slots, wide)
-    passed = swap(arrived)
-    own_a = gate_up(arrived, both)
+
+    groups = [
+        [(group ^ (e // 2 % 2)) * owners + e for e in range(owners)] for group in range(2)
+    ]
+
+    def dispatch(rows):
+        slots, wide = rows.shape
+        return lax.all_to_all(
+            rows.reshape(owners, MAIN, wide),
+            ("y", "exp"),
+            split_axis=0,
+            concat_axis=0,
+            axis_index_groups=groups,
+            tiled=True,
+        ).reshape(slots, wide)
+
+    one = dispatch(one)
+    far_one = swap(one)
+    two = dispatch(two)
+    far_two = swap(two)
+    early, left_top, right_bottom = lax.optimization_barrier((two, left_top, right_bottom))
+    own_a = gate_up(one, early, both)
+    own_a, left_top, right_bottom = lax.optimization_barrier((own_a, left_top, right_bottom))
     far_b = swap(own_a)
-    far_a = gate_up(passed, both)
+    beyond = (ring(left_top, 1), ring(right_bottom, -1))
+    far_two, far_b, left_bottom, right_top = lax.optimization_barrier(
+        (far_two, far_b, left_bottom, right_top)
+    )
+    far_a = gate_up(far_one, far_two, both)
     own_b = swap(far_a)
-    out = down(place, own_a, own_b, far_a, far_b, lower)
+    lower = (*here, left_top, left_bottom, right_top, right_bottom, *beyond)
+    out = down(place, (own_a, own_b, far_a, far_b), lower)
     back = lax.all_to_all(
         out.reshape(2 * owners, MAIN, out.shape[2]),
         ("y", "exp"),

time: 297 us -> 289 us (0.973)
  blocking collectives: 83 us -> 59 us
  waiting for transfers between devices: 101 us -> 117 us
  starting transfers between devices: 18.6 us -> 33.9 us
  local copies, waits for them, and re-layouts: 25.7 us -> 11 us
  other arithmetic: 4.28 us -> 1.16 us
    all_to_all x1, blocking collectives: 71.3 us -> 47.3 us  [dispatch(): lax.all_to_all(rows.reshape(owners, MAIN, wide), ('y', 'exp'), split_axis...]
    all_to_all x0 -> x1, waiting for transfers between devices: none -> 19.7 us  [dispatch(): lax.all_to_all(rows.reshape(owners, MAIN, wide), ('y', 'exp'), split_axis...]
    all_gather x1 -> x0, local copies, waits for them, and re-layouts: 16.7 us -> none  [per_device(): both = lax.all_gather(both, 'x', axis=0)]
    ppermute x0 -> x6, waiting for transfers between devices: none -> 10.2 us  [ring(): return lax.ppermute(x, 'x', [(i, (i + ahead) % 4) for i in range(4)])]
    all_gather x2 -> x1, waiting for transfers between devices: 14.9 us -> 6 us  [per_device(): lax.all_gather(both, 'x', axis=0, tiled=True)]
    ppermute x3 -> x4, waiting for transfers between devices: 21.1 us -> 15.7 us  [swap(): return lax.ppermute(x, 'y', [(0, 1), (1, 0)])]
    ppermute x0 -> x6, starting transfers between devices: none -> 5.36 us  [ring(): return lax.ppermute(x, 'x', [(i, (i + ahead) % 4) for i in range(4)])]
    ppermute x3 -> x4, starting transfers between devices: 4.63 us -> 9.49 us  [swap(): return lax.ppermute(x, 'y', [(0, 1), (1, 0)])]
  transfers between devices with their start and end apart: 7 -> 14, of which waited for: 5 -> 9; matrix products, arithmetic and copies ran while one was open for 7% -> 1% of each run, Pallas kernels for 13% -> 12%
where the time goes in v2:
time: 289 us; the launch traced here: 288 us
  waiting for transfers between devices  117 us (40%)
  blocking collectives  59 us (20%)
  Pallas kernels  52.4 us (18%)
  starting transfers between devices  33.9 us (12%)
  between operations  13.5 us (5%)
  local copies, waits for them, and re-layouts  11 us (4%)
    all_to_all x1, waiting for transfers between devices, per_device(): lax.all_to_all(out.reshape(2 * owners, MAIN, out.shape[2]), ('y', 'exp'),...  56.4 us
    all_to_all x1, blocking collectives, dispatch(): lax.all_to_all(rows.reshape(owners, MAIN, wide), ('y', 'exp'), split_axis...  47.3 us
    all_to_all x1, waiting for transfers between devices, dispatch(): lax.all_to_all(rows.reshape(owners, MAIN, wide), ('y', 'exp'), split_axis...  19.7 us
    pallas_call x1, Pallas kernels, attend(): pl.pallas_call(attend_kernel, grid_spec=pltpu.PrefetchScalarGridSpec(num_...  16.8 us
    ppermute x4, waiting for transfers between devices, swap(): return lax.ppermute(x, 'y', [(0, 1), (1, 0)])  15.7 us
    pallas_call x2, Pallas kernels, gate_up(): pl.pallas_call(gate_up_kernel, grid=(shards,), in_specs=[pl.BlockSpec(one...  15.1 us
    all_to_all x1, starting transfers between devices, per_device(): lax.all_to_all(out.reshape(2 * owners, MAIN, out.shape[2]), ('y', 'exp'),...  11.9 us
    all_gather x1, blocking collectives, per_device(): own_kv = lax.all_gather(kv, 'x', axis=0, tiled=True)  11.7 us
  transfers between devices with their start and end apart: 14, of which 9 were waited for; matrix products, arithmetic and copies ran while one was open for 1% of the time, Pallas kernels for 12%

profile of v2, /device:TPU:17, one launch (start us, length us, event | category | flops | bytes accessed | tf_op | source)
XLA Modules:
  0.0 287.8 jit_solution(2738231590722787082)
XLA Ops:
  6.5 4.6 %pack_weights.1 = bf16[4096,384]{1,0:T(8,128)(2,1)} custom-call(bf16[192,4096]{1,0:T(8,128)(2,1)} %bitcast.46, bf16[192,4096]{1,0:T(8,128)(2,1)} %bitcast.47), custom_call_target="tpu_custom_call" | custom-call | tf_op jit(solution)/shard_map/pack_weights/pallas_call | solution.py:89
  11.2 0.0 all-gather.2.cloned.1.call-update
  11.2 0.0 copy-start.3
  11.2 0.0 copy-start.7
  11.2 0.0 copy-start.8
  11.2 0.6 copy-done.10
  11.8 0.3 fusion.2
  12.1 0.7 pad_maximum_fusion
  12.9 1.7 pack_kv.1
  14.6 11.7 %all_gather.6.own_k_ref.own_v_ref = bf16[512,512]{1,0:T(8,128)(2,1)S(1)} all-gather(bf16[128,512]{1,0:T(8,128)(2,1)} %pack_kv.1), channel_id=1, replica_groups=mesh['y'=2,'x'=4,'exp'=32] {'x'}, dimensions={0}, use_global_device_ids=true | all-gather | bytes 655360 | tf_op jit(solution)/shard_map/all_gather | solution.py:456
  26.3 2.9 %collective-permute-start = (bf16[512,512]{1,0:T(8,128)(2,1)S(1)}, bf16[512,512]{1,0:T(8,128)(2,1)S(1)}, u32[]{:S(2)}, u32[]{:S(2)}) collective-permute-start(bf16[512,512]{1,0:T(8,128)(2,1)S(1)} %all_gather.6.own_k_ref.own_v_ref), channel_id=1, source_target_pairs={{0,128},{1,129},{2,130},{3,131},{4,132},{5,133},{6,134},{7,135},{8... | collective-permute-start | bytes 1572872 | tf_op jit(solution)/shard_map/ppermute | solution.py:457
  29.2 0.1 pad_add_fusion.place_ref
  29.3 8.8 %collective-permute-done.far_k_ref.far_v_ref = bf16[512,512]{1,0:T(8,128)(2,1)S(1)} collective-permute-done((bf16[512,512]{1,0:T(8,128)(2,1)S(1)}, bf16[512,512]{1,0:T(8,128)(2,1)S(1)}, u32[]{:S(2)}, u32[]{:S(2)}) %collective-permute-start) | collective-permute-done | bytes 524320 | tf_op jit(solution)/shard_map/ppermute | solution.py:457
  38.1 0.8 copy-done.5
  38.9 0.8 copy-done.6
  39.8 16.8 %attend.1 = (f32[128,4096]{1,0:T(8,128)}, bf16[256,2560]{1,0:T(8,128)(2,1)S(1)}, bf16[256,2048]{1,0:T(8,128)(2,1)}) custom-call(s32[3]{0:T(128)S(1)} %pad_add_fusion.place_ref, bf16[128,4096]{1,0:T(8,128)(2,1)S(1)} %bitcast.40, bf16[512,512]{1,0:T(8,128)(2,1)S(1)} %all_gather.6.own_k_ref.own_v_ref, bf16[512,512]{1,0:T(8,128)(2,1)S(1)} %all_gather.6.own_k_ref.own_v_ref, ...), custom_call_target="tpu_custom_call" | custom-call | tf_op jit(solution)/shard_map/attend/pallas_call | solution.py:186
  56.6 47.3 %all_to_all.15 = bf16[32,8,2560]{2,1,0:T(8,128)(2,1)S(1)} all-to-all(bf16[32,8,2560]{2,1,0:T(8,128)(2,1)S(1)} %bitcast.39), channel_id=1, replica_groups={{0,1,130,131,4,5,134,135,8,9,138,139,12,13,142,143,16,17,146,147,20,21,..., dimensions={0} | all-to-all | bytes 2621440 | tf_op jit(solution)/shard_map/all_to_all | solution.py:477
  103.9 4.2 %all-to-all-start.1 = ((bf16[32,8,2048]{2,1,0:T(8,128)(2,1)}), bf16[32,8,2048]{2,1,0:T(8,128)(2,1)S(1)}, u32[]{:S(2)}, u32[]{:S(2)}) async-start(bf16[32,8,2048]{2,1,0:T(8,128)(2,1)} %bitcast.15), calls=%async_computation.1 | async-start | bytes 2097152 | tf_op jit(solution)/shard_map/all_to_all | solution.py:477
  108.1 2.4 slice_bitcast_fusion
  110.5 0.0 collective-permute-start.1
  110.5 2.7 collective-permute-start.2
  113.1 4.2 %collective-permute-start.3 = (bf16[256,2560]{1,0:T(8,128)(2,1)S(1)}, bf16[256,2560]{1,0:T(8,128)(2,1)}, u32[]{:S(2)}, u32[]{:S(2)}) collective-permute-start(bf16[256,2560]{1,0:T(8,128)(2,1)S(1)} %bitcast.35), channel_id=1, source_target_pairs={{0,128},{128,0},{1,129},{129,1},{2,130},{130,2},{3,131},{131,3},{4... | collective-permute-start | bytes 3932168 | tf_op jit(solution)/shard_map/ppermute | solution.py:426
  117.3 19.7 %all-to-all-done.1 = bf16[32,8,2048]{2,1,0:T(8,128)(2,1)S(1)} async-done(((bf16[32,8,2048]{2,1,0:T(8,128)(2,1)}), bf16[32,8,2048]{2,1,0:T(8,128)(2,1)S(1)}, u32[]{:S(2)}, u32[]{:S(2)}) %all-to-all-start.1) | async-done | bytes 1048608 | tf_op jit(solution)/shard_map/all_to_all | solution.py:477
  137.0 4.2 %collective-permute-start.4 = (bf16[256,2048]{1,0:T(8,128)(2,1)S(1)}, bf16[256,2048]{1,0:T(8,128)(2,1)}, u32[]{:S(2)}, u32[]{:S(2)}) collective-permute-start(bf16[256,2048]{1,0:T(8,128)(2,1)S(1)} %bitcast.37), channel_id=1, source_target_pairs={{0,128},{128,0},{1,129},{129,1},{2,130},{130,2},{3,131},{131,3},{4... | collective-permute-start | bytes 3145736 | tf_op jit(solution)/shard_map/ppermute | solution.py:426
  141.2 0.0 collective-permute-start.6
  141.2 6.9 %collective-permute-done.1.refs_2_ = bf16[768,512]{1,0:T(8,128)(2,1)} collective-permute-done((bf16[768,512]{1,0:T(8,128)(2,1)}, bf16[768,512]{1,0:T(8,128)(2,1)}, u32[]{:S(2)}, u32[]{:S(2)}) %collective-permute-start.1) | collective-permute-done | bytes 786464 | tf_op jit(solution)/shard_map/ppermute | solution.py:430
  148.1 0.0 collective-permute-start.7
  148.1 0.0 collective-permute-done.2.refs_5_
  148.1 6.0 %all-gather.2.cloned.1.call-done = bf16[16384,384]{1,0:T(8,128)(2,1)} async-done(((bf16[4096,384]{1,0:T(8,128)(2,1)}), bf16[16384,384]{1,0:T(8,128)(2,1)}) %all-gather.2.cloned.1.call-update) | async-done | bytes 12582928 | tf_op jit(solution)/shard_map/all_gather | solution.py:460
  154.1 4.6 %copy-done = bf16[16384,384]{1,0:T(8,128)(2,1)S(1)} copy-done((bf16[16384,384]{1,0:T(8,128)(2,1)S(1)}, bf16[16384,384]{1,0:T(8,128)(2,1)}, u32[]{:S(2)}) %copy-start) | copy-done | bytes 12582936
  158.7 6.7 %gate_up.2.own_a = bf16[288,768]{1,0:T(8,128)(2,1)S(1)} custom-call(bf16[256,2560]{1,0:T(8,128)(2,1)S(1)} %bitcast.36, bf16[256,2048]{1,0:T(8,128)(2,1)S(1)} %bitcast.38, bf16[4,4096,384]{2,1,0:T(8,128)(2,1)S(1)} %bitcast.32), custom_call_target="tpu_custom_call" | custom-call | flops 3623878656 | bytes 14942208 | tf_op jit(solution)/shard_map/gate_up/pallas_call | solution.py:262
  165.4 0.1 collective-permute-start.5
  165.5 2.6 collective-permute-done.6.refs_3_
  168.1 0.0 collective-permute-start.9
  168.1 0.0 collective-permute-done.7.refs_4_
  168.1 2.7 collective-permute-start.10
  170.8 7.0 %collective-permute-done.5.far_b = bf16[288,768]{1,0:T(8,128)(2,1)S(1)} collective-permute-done((bf16[288,768]{1,0:T(8,128)(2,1)S(1)}, bf16[288,768]{1,0:T(8,128)(2,1)S(1)}, u32[]{:S(2)}, u32[]{:S(2)}) %collective-permute-start.5) | collective-permute-done | bytes 442400 | tf_op jit(solution)/shard_map/ppermute | solution.py:426
  177.8 8.4 %gate_up.3.far_a = bf16[288,768]{1,0:T(8,128)(2,1)S(1)} custom-call(bf16[256,2560]{1,0:T(8,128)(2,1)} %collective-permute-done.3.one_ref, bf16[256,2048]{1,0:T(8,128)(2,1)} %collective-permute-done.4.two_ref, bf16[4,4096,384]{2,1,0:T(8,128)(2,1)S(1)} %bitcast.33), custom_call_target="tpu_custom_call" | custom-call | flops 3623878656 | bytes 14942208 | tf_op jit(solution)/shard_map/gate_up/pallas_call | solution.py:262
  186.1 1.0 collective-permute-start.8
  187.1 0.8 collective-permute-done.9.refs_6_
  187.9 8.7 %collective-permute-done.8.own_b = bf16[288,768]{1,0:T(8,128)(2,1)S(1)} collective-permute-done((bf16[288,768]{1,0:T(8,128)(2,1)S(1)}, bf16[288,768]{1,0:T(8,128)(2,1)S(1)}, u32[]{:S(2)}, u32[]{:S(2)}) %collective-permute-start.8) | collective-permute-done | bytes 442400 | tf_op jit(solution)/shard_map/ppermute | solution.py:426
  196.6 10.1 %down.1 = bf16[2,256,2304]{2,1,0:T(8,128)(2,1)} custom-call(s32[3]{0:T(128)S(1)} %pad_add_fusion.place_ref, bf16[288,768]{1,0:T(8,128)(2,1)S(1)} %gate_up.2.own_a, bf16[288,768]{1,0:T(8,128)(2,1)S(1)} %collective-permute-done.8.own_b, bf16[288,768]{1,0:T(8,128)(2,1)S(1)} %gate_up.3.far_a, bf16[288,768]{1,0:T(8,128)(2,1)S(1)} %collective-permute-done.5.far_b, ...), custom_call_target="tpu_custom_call" | custom-call | tf_op jit(solution)/shard_map/down/pallas_call | solution.py:346
  206.8 11.9 %all-to-all-start.2 = ((bf16[64,8,2304]{2,1,0:T(8,128)(2,1)}), bf16[64,8,2304]{2,1,0:T(8,128)(2,1)S(1)}, u32[]{:S(2)}, u32[]{:S(2)}) async-start(bf16[64,8,2304]{2,1,0:T(8,128)(2,1)} %bitcast.24), calls=%async_computation.2 | async-start | bytes 4718592 | tf_op jit(solution)/shard_map/all_to_all | solution.py:502
  218.7 0.1 copy.12
  218.8 0.1 copy.13
  218.9 56.4 %all-to-all-done.2 = bf16[64,8,2304]{2,1,0:T(8,128)(2,1)S(1)} async-done(((bf16[64,8,2304]{2,1,0:T(8,128)(2,1)}), bf16[64,8,2304]{2,1,0:T(8,128)(2,1)S(1)}, u32[]{:S(2)}, u32[]{:S(2)}) %all-to-all-start.2) | async-done | bytes 2359328 | tf_op jit(solution)/shard_map/all_to_all | solution.py:502
  275.4 1.6 copy-done.2
  277.0 4.0 %combine.1 = bf16[128,4096]{1,0:T(8,128)(2,1)} custom-call(s32[128,8]{1,0:T(8,128)S(1)} %bitcast.42, f32[128,8]{1,0:T(8,128)S(1)} %bitcast.43, f32[128,4096]{1,0:T(8,128)S(1)} %copy-done.2, bf16[2,256,2304]{2,1,0:T(8,128)(2,1)S(1)} %bitcast.34), custom_call_target="tpu_custom_call" | custom-call | tf_op jit(solution)/shard_map/combine/pallas_call | solution.py:409
  (20 shorter events, 0.1 us)
Async XLA Ops:
  6.5 147.6 %all-gather.2.cloned.1.call-start = ((), (), s32[]{:S(2)}) async-start(), calls=%async_computation.3 | async-start | bytes 15728640 | tf_op jit(solution)/shard_map/all_gather | solution.py:460
  11.2 0.7 copy-start.10
  11.2 26.9 %copy-start.4 = (bf16[1,128,4096]{2,1,0:T(8,128)(2,1)S(1)}, bf16[1,128,4096]{2,1,0:T(8,128)(2,1)}, u32[]{:S(2)}) copy-start(bf16[1,128,4096]{2,1,0:T(8,128)(2,1)} %param.15) | copy-start | bytes 3145732
  11.2 26.9 %copy-start.3 = (bf16[1,128,4096]{2,1,0:T(8,128)(2,1)S(1)}, bf16[1,128,4096]{2,1,0:T(8,128)(2,1)}, u32[]{:S(2)}) copy-start(bf16[1,128,4096]{2,1,0:T(8,128)(2,1)} %param.11) | copy-start | bytes 3145732
  11.2 26.9 %copy-start.7 = (f32[4096]{0:T(1024)S(1)}, f32[4096]{0:T(1024)}, u32[]{:S(2)}) copy-start(f32[4096]{0:T(1024)} %param.16) | copy-start | bytes 49156
  11.2 26.9 %copy-start.8 = (s32[1,128,8]{1,2,0:T(8,128)S(1)}, s32[1,128,8]{1,2,0:T(8,128)}, u32[]{:S(2)}) copy-start(s32[1,128,8]{1,2,0:T(8,128)} %param.17) | copy-start | bytes 12292
  26.3 11.8 %collective-permute-start = (bf16[512,512]{1,0:T(8,128)(2,1)S(1)}, bf16[512,512]{1,0:T(8,128)(2,1)S(1)}, u32[]{:S(2)}, u32[]{:S(2)}) collective-permute-start(bf16[512,512]{1,0:T(8,128)(2,1)S(1)} %all_gather.6.own_k_ref.own_v_ref), channel_id=1, source_target_pairs={{0,128},{1,129},{2,130},{3,131},{4,132},{5,133},{6,134},{7,135},{8... | collective-permute-start | bytes 1572872 | tf_op jit(solution)/shard_map/ppermute | solution.py:457
  38.1 0.8 copy-start.5
  38.9 0.8 copy-start.6
  103.9 33.1 %all-to-all-start.1 = ((bf16[32,8,2048]{2,1,0:T(8,128)(2,1)}), bf16[32,8,2048]{2,1,0:T(8,128)(2,1)S(1)}, u32[]{:S(2)}, u32[]{:S(2)}) async-start(bf16[32,8,2048]{2,1,0:T(8,128)(2,1)} %bitcast.15), calls=%async_computation.1 | async-start | bytes 2097152 | tf_op jit(solution)/shard_map/all_to_all | solution.py:477
  110.5 37.6 %collective-permute-start.1 = (bf16[768,512]{1,0:T(8,128)(2,1)}, bf16[768,512]{1,0:T(8,128)(2,1)}, u32[]{:S(2)}, u32[]{:S(2)}) collective-permute-start(bf16[768,512]{1,0:T(8,128)(2,1)} %get-tuple-element.32.refs_0_), channel_id=1, source_target_pairs={{0,32},{32,64},{64,96},{96,0},{1,33},{33,65},{65,97},{97,1},{2,34}... | collective-permute-start | bytes 2359304 | tf_op jit(solution)/shard_map/ppermute | solution.py:430
  110.5 37.6 %collective-permute-start.2 = (bf16[768,512]{1,0:T(8,128)(2,1)S(1)}, bf16[768,512]{1,0:T(8,128)(2,1)}, u32[]{:S(2)}, u32[]{:S(2)}) collective-permute-start(bf16[768,512]{1,0:T(8,128)(2,1)S(1)} %get-tuple-element.31.refs_1_), channel_id=1, source_target_pairs={{0,96},{32,0},{64,32},{96,64},{1,97},{33,1},{65,33},{97,65},{2,98}... | collective-permute-start | bytes 2359304 | tf_op jit(solution)/shard_map/ppermute | solution.py:430
  113.1 64.6 %collective-permute-start.3 = (bf16[256,2560]{1,0:T(8,128)(2,1)S(1)}, bf16[256,2560]{1,0:T(8,128)(2,1)}, u32[]{:S(2)}, u32[]{:S(2)}) collective-permute-start(bf16[256,2560]{1,0:T(8,128)(2,1)S(1)} %bitcast.35), channel_id=1, source_target_pairs={{0,128},{128,0},{1,129},{129,1},{2,130},{130,2},{3,131},{131,3},{4... | collective-permute-start | bytes 3932168 | tf_op jit(solution)/shard_map/ppermute | solution.py:426
  137.0 33.7 %collective-permute-start.4 = (bf16[256,2048]{1,0:T(8,128)(2,1)S(1)}, bf16[256,2048]{1,0:T(8,128)(2,1)}, u32[]{:S(2)}, u32[]{:S(2)}) collective-permute-start(bf16[256,2048]{1,0:T(8,128)(2,1)S(1)} %bitcast.37), channel_id=1, source_target_pairs={{0,128},{128,0},{1,129},{129,1},{2,130},{130,2},{3,131},{131,3},{4... | collective-permute-start | bytes 3145736 | tf_op jit(solution)/shard_map/ppermute | solution.py:426
  141.2 26.8 %collective-permute-start.6 = (bf16[768,512]{1,0:T(8,128)(2,1)S(1)}, bf16[768,512]{1,0:T(8,128)(2,1)}, u32[]{:S(2)}, u32[]{:S(2)}) collective-permute-start(bf16[768,512]{1,0:T(8,128)(2,1)S(1)} %get-tuple-element.31.refs_1_), channel_id=1, source_target_pairs={{0,32},{32,64},{64,96},{96,0},{1,33},{33,65},{65,97},{97,1},{2,34}... | collective-permute-start | bytes 2359304 | tf_op jit(solution)/shard_map/ppermute | solution.py:430
  148.1 20.0 %collective-permute-start.7 = (bf16[768,512]{1,0:T(8,128)(2,1)}, bf16[768,512]{1,0:T(8,128)(2,1)}, u32[]{:S(2)}, u32[]{:S(2)}) collective-permute-start(bf16[768,512]{1,0:T(8,128)(2,1)} %get-tuple-element.32.refs_0_), channel_id=1, source_target_pairs={{0,96},{32,0},{64,32},{96,64},{1,97},{33,1},{65,33},{97,65},{2,98}... | collective-permute-start | bytes 2359304 | tf_op jit(solution)/shard_map/ppermute | solution.py:430
  154.1 4.6 %copy-start = (bf16[16384,384]{1,0:T(8,128)(2,1)S(1)}, bf16[16384,384]{1,0:T(8,128)(2,1)}, u32[]{:S(2)}) copy-start(bf16[16384,384]{1,0:T(8,128)(2,1)} %all-gather.2.cloned.1.call-done) | copy-start | bytes 37748740
  158.7 19.1 %copy-start.1 = (bf16[16384,384]{1,0:T(8,128)(2,1)S(1)}, bf16[16384,384]{1,0:T(8,128)(2,1)}, u32[]{:S(2)}) copy-start(bf16[16384,384]{1,0:T(8,128)(2,1)} %all-gather.2.cloned.1.call-done) | copy-start | bytes 37748740
  165.4 12.3 %collective-permute-start.5 = (bf16[288,768]{1,0:T(8,128)(2,1)S(1)}, bf16[288,768]{1,0:T(8,128)(2,1)S(1)}, u32[]{:S(2)}, u32[]{:S(2)}) collective-permute-start(bf16[288,768]{1,0:T(8,128)(2,1)S(1)} %gate_up.2.own_a), channel_id=1, source_target_pairs={{0,128},{128,0},{1,129},{129,1},{2,130},{130,2},{3,131},{131,3},{4... | collective-permute-start | bytes 1327112 | tf_op jit(solution)/shard_map/ppermute | solution.py:426
  168.1 19.8 %collective-permute-start.9 = (bf16[768,512]{1,0:T(8,128)(2,1)}, bf16[768,512]{1,0:T(8,128)(2,1)S(1)}, u32[]{:S(2)}, u32[]{:S(2)}) collective-permute-start(bf16[768,512]{1,0:T(8,128)(2,1)} %collective-permute-done.1.refs_2_), channel_id=1, source_target_pairs={{0,32},{32,64},{64,96},{96,0},{1,33},{33,65},{65,97},{97,1},{2,34}... | collective-permute-start | bytes 2359304 | tf_op jit(solution)/shard_map/ppermute | solution.py:430
  168.1 19.8 %collective-permute-start.10 = (bf16[768,512]{1,0:T(8,128)(2,1)}, bf16[768,512]{1,0:T(8,128)(2,1)S(1)}, u32[]{:S(2)}, u32[]{:S(2)}) collective-permute-start(bf16[768,512]{1,0:T(8,128)(2,1)} %collective-permute-done.2.refs_5_), channel_id=1, source_target_pairs={{0,96},{32,0},{64,32},{96,64},{1,97},{33,1},{65,33},{97,65},{2,98}... | collective-permute-start | bytes 2359304 | tf_op jit(solution)/shard_map/ppermute | solution.py:430
  186.1 10.5 %collective-permute-start.8 = (bf16[288,768]{1,0:T(8,128)(2,1)S(1)}, bf16[288,768]{1,0:T(8,128)(2,1)S(1)}, u32[]{:S(2)}, u32[]{:S(2)}) collective-permute-start(bf16[288,768]{1,0:T(8,128)(2,1)S(1)} %gate_up.3.far_a), channel_id=1, source_target_pairs={{0,128},{128,0},{1,129},{129,1},{2,130},{130,2},{3,131},{131,3},{4... | collective-permute-start | bytes 1327112 | tf_op jit(solution)/shard_map/ppermute | solution.py:426
  206.8 12.1 %copy-start.9 = (f32[1,128,8]{1,2,0:T(8,128)S(1)}, f32[1,128,8]{1,2,0:T(8,128)}, u32[]{:S(2)}) copy-start(f32[1,128,8]{1,2,0:T(8,128)} %param.18) | copy-start | bytes 12292
  206.8 68.6 %all-to-all-start.2 = ((bf16[64,8,2304]{2,1,0:T(8,128)(2,1)}), bf16[64,8,2304]{2,1,0:T(8,128)(2,1)S(1)}, u32[]{:S(2)}, u32[]{:S(2)}) async-start(bf16[64,8,2304]{2,1,0:T(8,128)(2,1)} %bitcast.24), calls=%async_computation.2 | async-start | bytes 4718592 | tf_op jit(solution)/shard_map/all_to_all | solution.py:502
  275.4 1.6 copy-start.2
Sparse Core Ops, SparseCore 0:
  11.3 142.7 all-gather.1

commit v3 on v2

--- a/solution.py
+++ b/solution.py
@@ -15,7 +15,7 @@
 TOP = 8
 HALF = HEAD_DIM // 2
 STEP_HEADS = 4
-FIRST = 5
+FIRST = 6
 MAIN = 8
 
 F32 = jnp.float32

time: 289 us -> 291 us (level)
  blocking collectives: 59 us -> 64.5 us
  waiting for transfers between devices: 117 us -> 114 us
    ppermute x6, waiting for transfers between devices: 10.2 us -> 30.7 us  [ring(): return lax.ppermute(x, 'x', [(i, (i + ahead) % 4) for i in range(4)])]
    all_to_all x1, waiting for transfers between devices: 19.7 us -> 0.01 us  [dispatch(): lax.all_to_all(rows.reshape(owners, MAIN, wide), ('y', 'exp'), split_axis...]
    all_gather x1, waiting for transfers between devices: 6 us -> 0.01 us  [per_device(): lax.all_gather(both, 'x', axis=0, tiled=True)]
    all_to_all x1, blocking collectives: 47.3 us -> 52.8 us  [dispatch(): lax.all_to_all(rows.reshape(owners, MAIN, wide), ('y', 'exp'), split_axis...]
    unnamed x24 -> x26, local copies, waits for them, and re-layouts: 8.65 us -> 8.65 us
  transfers between devices with their start and end apart: 14 -> 14, of which waited for: 9 -> 7; matrix products, arithmetic and copies ran while one was open for 1% -> 1% of each run, Pallas kernels for 12% -> 11%
where the time goes in v3:
time: 291 us
  waiting for transfers between devices  114 us (39%)
  blocking collectives  64.5 us (22%)
  Pallas kernels  52 us (18%)
  starting transfers between devices  34.2 us (12%)
  between operations  13.5 us (5%)
  local copies, waits for them, and re-layouts  11 us (4%)
    all_to_all x1, waiting for transfers between devices, per_device(): lax.all_to_all(out.reshape(2 * owners, MAIN, out.shape[2]), ('y', 'exp'),...  56.4 us
    all_to_all x1, blocking collectives, dispatch(): lax.all_to_all(rows.reshape(owners, MAIN, wide), ('y', 'exp'), split_axis...  52.8 us
    ppermute x6, waiting for transfers between devices, ring(): return lax.ppermute(x, 'x', [(i, (i + ahead) % 4) for i in range(4)])  30.7 us
    ppermute x4, waiting for transfers between devices, swap(): return lax.ppermute(x, 'y', [(0, 1), (1, 0)])  18.4 us
    pallas_call x1, Pallas kernels, attend(): pl.pallas_call(attend_kernel, grid_spec=pltpu.PrefetchScalarGridSpec(num_...  16.5 us
    pallas_call x2, Pallas kernels, gate_up(): pl.pallas_call(gate_up_kernel, grid=(shards,), in_specs=[pl.BlockSpec(one...  15.1 us
    all_to_all x1, starting transfers between devices, per_device(): lax.all_to_all(out.reshape(2 * owners, MAIN, out.shape[2]), ('y', 'exp'),...  12.3 us
    all_gather x1, blocking collectives, per_device(): own_kv = lax.all_gather(kv, 'x', axis=0, tiled=True)  11.7 us
  transfers between devices with their start and end apart: 14, of which 7 were waited for; matrix products, arithmetic and copies ran while one was open for 1% of the time, Pallas kernels for 11%

profile of v3, /device:TPU:17, one launch (start us, length us, event | category | flops | bytes accessed | tf_op | source)
XLA Modules:
  0.0 290.6 jit_solution(526335763531037445)
XLA Ops:
  6.5 4.6 %pack_weights.1 = bf16[4096,384]{1,0:T(8,128)(2,1)} custom-call(bf16[192,4096]{1,0:T(8,128)(2,1)} %bitcast.47, bf16[192,4096]{1,0:T(8,128)(2,1)} %bitcast.48), custom_call_target="tpu_custom_call" | custom-call | tf_op jit(solution)/shard_map/pack_weights/pallas_call | solution.py:89
  11.2 0.0 all-gather.2.cloned.1.call-update
  11.2 0.0 copy-start.3
  11.2 0.0 copy-start.8
  11.2 0.0 copy-start.9
  11.2 0.6 copy-done.11
  11.8 0.3 fusion.2
  12.1 0.7 pad_maximum_fusion
  12.9 1.7 pack_kv.1
  14.6 11.7 %all_gather.6.own_k_ref.own_v_ref = bf16[512,512]{1,0:T(8,128)(2,1)S(1)} all-gather(bf16[128,512]{1,0:T(8,128)(2,1)} %pack_kv.1), channel_id=1, replica_groups=mesh['y'=2,'x'=4,'exp'=32] {'x'}, dimensions={0}, use_global_device_ids=true | all-gather | bytes 655360 | tf_op jit(solution)/shard_map/all_gather | solution.py:456
  26.3 2.9 %collective-permute-start = (bf16[512,512]{1,0:T(8,128)(2,1)S(1)}, bf16[512,512]{1,0:T(8,128)(2,1)S(1)}, u32[]{:S(2)}, u32[]{:S(2)}) collective-permute-start(bf16[512,512]{1,0:T(8,128)(2,1)S(1)} %all_gather.6.own_k_ref.own_v_ref), channel_id=1, source_target_pairs={{0,128},{1,129},{2,130},{3,131},{4,132},{5,133},{6,134},{7,135},{8... | collective-permute-start | bytes 1572872 | tf_op jit(solution)/shard_map/ppermute | solution.py:457
  29.2 0.1 pad_add_fusion.place_ref
  29.3 8.8 %collective-permute-done.far_k_ref.far_v_ref = bf16[512,512]{1,0:T(8,128)(2,1)S(1)} collective-permute-done((bf16[512,512]{1,0:T(8,128)(2,1)S(1)}, bf16[512,512]{1,0:T(8,128)(2,1)S(1)}, u32[]{:S(2)}, u32[]{:S(2)}) %collective-permute-start) | collective-permute-done | bytes 524320 | tf_op jit(solution)/shard_map/ppermute | solution.py:457
  38.1 0.8 copy-done.6
  38.9 0.8 copy-done.7
  39.7 16.5 %attend.1 = (f32[128,4096]{1,0:T(8,128)}, bf16[256,3072]{1,0:T(8,128)(2,1)S(1)}, bf16[256,1536]{1,0:T(8,128)(2,1)S(1)}) custom-call(s32[3]{0:T(128)S(1)} %pad_add_fusion.place_ref, bf16[128,4096]{1,0:T(8,128)(2,1)S(1)} %bitcast.40, bf16[512,512]{1,0:T(8,128)(2,1)S(1)} %all_gather.6.own_k_ref.own_v_ref, bf16[512,512]{1,0:T(8,128)(2,1)S(1)} %all_gather.6.own_k_ref.own_v_ref, ...), custom_call_target="tpu_custom_call" | custom-call | tf_op jit(solution)/shard_map/attend/pallas_call | solution.py:186
  56.2 52.8 %all_to_all.15 = bf16[32,8,3072]{2,1,0:T(8,128)(2,1)S(1)} all-to-all(bf16[32,8,3072]{2,1,0:T(8,128)(2,1)S(1)} %bitcast.39), channel_id=1, replica_groups={{0,1,130,131,4,5,134,135,8,9,138,139,12,13,142,143,16,17,146,147,20,21,..., dimensions={0} | all-to-all | bytes 3145728 | tf_op jit(solution)/shard_map/all_to_all | solution.py:477
  109.0 4.3 %all-to-all-start.1 = ((bf16[32,8,1536]{2,1,0:T(8,128)(2,1)}), bf16[32,8,1536]{2,1,0:T(8,128)(2,1)S(1)}, u32[]{:S(2)}, u32[]{:S(2)}) async-start(bf16[32,8,1536]{2,1,0:T(8,128)(2,1)} %bitcast.42), calls=%async_computation.1 | async-start | bytes 1572864 | tf_op jit(solution)/shard_map/all_to_all | solution.py:477
  113.3 2.3 slice_bitcast_fusion
  115.7 0.0 collective-permute-start.1
  115.7 3.9 %collective-permute-start.3 = (bf16[256,3072]{1,0:T(8,128)(2,1)S(1)}, bf16[256,3072]{1,0:T(8,128)(2,1)}, u32[]{:S(2)}, u32[]{:S(2)}) collective-permute-start(bf16[256,3072]{1,0:T(8,128)(2,1)S(1)} %bitcast.35), channel_id=1, source_target_pairs={{0,128},{128,0},{1,129},{129,1},{2,130},{130,2},{3,131},{131,3},{4... | collective-permute-start | bytes 4718600 | tf_op jit(solution)/shard_map/ppermute | solution.py:426
  119.6 2.7 collective-permute-start.2
  122.3 0.0 collective-permute-start.6
  122.3 2.7 collective-permute-start.7
  125.0 26.2 %collective-permute-done.1.refs_2_ = bf16[768,512]{1,0:T(8,128)(2,1)} collective-permute-done((bf16[768,512]{1,0:T(8,128)(2,1)}, bf16[768,512]{1,0:T(8,128)(2,1)}, u32[]{:S(2)}, u32[]{:S(2)}) %collective-permute-start.1) | collective-permute-done | bytes 786464 | tf_op jit(solution)/shard_map/ppermute | solution.py:430
  151.2 0.0 all-to-all-done.1
  151.2 0.9 collective-permute-start.4
  152.1 0.0 collective-permute-done.2.refs_5_
  152.1 4.6 %copy-done = bf16[16384,384]{1,0:T(8,128)(2,1)S(1)} copy-done((bf16[16384,384]{1,0:T(8,128)(2,1)S(1)}, bf16[16384,384]{1,0:T(8,128)(2,1)}, u32[]{:S(2)}) %copy-start) | copy-done | bytes 12582936
  156.7 6.7 %gate_up.2.own_a = bf16[288,768]{1,0:T(8,128)(2,1)S(1)} custom-call(bf16[256,3072]{1,0:T(8,128)(2,1)S(1)} %bitcast.36, bf16[256,1536]{1,0:T(8,128)(2,1)S(1)} %bitcast.38, bf16[4,4096,384]{2,1,0:T(8,128)(2,1)S(1)} %bitcast.32), custom_call_target="tpu_custom_call" | custom-call | flops 3623878656 | bytes 14942208 | tf_op jit(solution)/shard_map/gate_up/pallas_call | solution.py:262
  163.5 0.7 collective-permute-start.5
  164.2 3.9 %collective-permute-done.6.refs_3_ = bf16[768,512]{1,0:T(8,128)(2,1)} collective-permute-done((bf16[768,512]{1,0:T(8,128)(2,1)S(1)}, bf16[768,512]{1,0:T(8,128)(2,1)}, u32[]{:S(2)}, u32[]{:S(2)}) %collective-permute-start.6) | collective-permute-done | bytes 786464 | tf_op jit(solution)/shard_map/ppermute | solution.py:430
  168.1 0.5 collective-permute-done.7.refs_4_
  168.6 2.1 collective-permute-start.10
  170.8 0.0 collective-permute-done.4.two_ref
  170.8 9.4 %collective-permute-done.5.far_b = bf16[288,768]{1,0:T(8,128)(2,1)S(1)} collective-permute-done((bf16[288,768]{1,0:T(8,128)(2,1)S(1)}, bf16[288,768]{1,0:T(8,128)(2,1)S(1)}, u32[]{:S(2)}, u32[]{:S(2)}) %collective-permute-start.5) | collective-permute-done | bytes 442400 | tf_op jit(solution)/shard_map/ppermute | solution.py:426
  180.1 0.0 collective-permute-done.3.one_ref
  180.1 8.4 %gate_up.3.far_a = bf16[288,768]{1,0:T(8,128)(2,1)S(1)} custom-call(bf16[256,3072]{1,0:T(8,128)(2,1)} %collective-permute-done.3.one_ref, bf16[256,1536]{1,0:T(8,128)(2,1)} %collective-permute-done.4.two_ref, bf16[4,4096,384]{2,1,0:T(8,128)(2,1)S(1)} %bitcast.33), custom_call_target="tpu_custom_call" | custom-call | flops 3623878656 | bytes 14942208 | tf_op jit(solution)/shard_map/gate_up/pallas_call | solution.py:262
  188.5 1.6 collective-permute-start.8
  190.0 0.0 collective-permute-done.9.refs_6_
  190.1 9.0 %collective-permute-done.8.own_b = bf16[288,768]{1,0:T(8,128)(2,1)S(1)} collective-permute-done((bf16[288,768]{1,0:T(8,128)(2,1)S(1)}, bf16[288,768]{1,0:T(8,128)(2,1)S(1)}, u32[]{:S(2)}, u32[]{:S(2)}) %collective-permute-start.8) | collective-permute-done | bytes 442400 | tf_op jit(solution)/shard_map/ppermute | solution.py:426
  199.1 10.1 %down.1 = bf16[2,256,2304]{2,1,0:T(8,128)(2,1)} custom-call(s32[3]{0:T(128)S(1)} %pad_add_fusion.place_ref, bf16[288,768]{1,0:T(8,128)(2,1)S(1)} %gate_up.2.own_a, bf16[288,768]{1,0:T(8,128)(2,1)S(1)} %collective-permute-done.8.own_b, bf16[288,768]{1,0:T(8,128)(2,1)S(1)} %gate_up.3.far_a, bf16[288,768]{1,0:T(8,128)(2,1)S(1)} %collective-permute-done.5.far_b, ...), custom_call_target="tpu_custom_call" | custom-call | tf_op jit(solution)/shard_map/down/pallas_call | solution.py:346
  209.2 12.3 %all-to-all-start.2 = ((bf16[64,8,2304]{2,1,0:T(8,128)(2,1)}), bf16[64,8,2304]{2,1,0:T(8,128)(2,1)S(1)}, u32[]{:S(2)}, u32[]{:S(2)}) async-start(bf16[64,8,2304]{2,1,0:T(8,128)(2,1)} %bitcast.24), calls=%async_computation.2 | async-start | bytes 4718592 | tf_op jit(solution)/shard_map/all_to_all | solution.py:502
  221.5 0.1 copy.12
  221.7 0.1 copy.13
  221.8 56.4 %all-to-all-done.2 = bf16[64,8,2304]{2,1,0:T(8,128)(2,1)S(1)} async-done(((bf16[64,8,2304]{2,1,0:T(8,128)(2,1)}), bf16[64,8,2304]{2,1,0:T(8,128)(2,1)S(1)}, u32[]{:S(2)}, u32[]{:S(2)}) %all-to-all-start.2) | async-done | bytes 2359328 | tf_op jit(solution)/shard_map/all_to_all | solution.py:502
  278.2 1.6 copy-done.2
  279.8 4.0 %combine.1 = bf16[128,4096]{1,0:T(8,128)(2,1)} custom-call(s32[128,8]{1,0:T(8,128)S(1)} %bitcast.43, f32[128,8]{1,0:T(8,128)S(1)} %bitcast.44, f32[128,4096]{1,0:T(8,128)S(1)} %copy-done.2, bf16[2,256,2304]{2,1,0:T(8,128)(2,1)S(1)} %bitcast.34), custom_call_target="tpu_custom_call" | custom-call | tf_op jit(solution)/shard_map/combine/pallas_call | solution.py:409
  (22 shorter events, 0.1 us)
Async XLA Ops:
  6.5 145.6 %all-gather.2.cloned.1.call-start = ((), (), s32[]{:S(2)}) async-start(), calls=%async_computation.3 | async-start | bytes 15728640 | tf_op jit(solution)/shard_map/all_gather | solution.py:460
  11.2 0.7 copy-start.11
  11.2 26.9 %copy-start.4 = (bf16[1,128,4096]{2,1,0:T(8,128)(2,1)S(1)}, bf16[1,128,4096]{2,1,0:T(8,128)(2,1)}, u32[]{:S(2)}) copy-start(bf16[1,128,4096]{2,1,0:T(8,128)(2,1)} %param.15) | copy-start | bytes 3145732
  11.2 26.9 %copy-start.3 = (bf16[1,128,4096]{2,1,0:T(8,128)(2,1)S(1)}, bf16[1,128,4096]{2,1,0:T(8,128)(2,1)}, u32[]{:S(2)}) copy-start(bf16[1,128,4096]{2,1,0:T(8,128)(2,1)} %param.11) | copy-start | bytes 3145732
  11.2 26.9 %copy-start.8 = (f32[4096]{0:T(1024)S(1)}, f32[4096]{0:T(1024)}, u32[]{:S(2)}) copy-start(f32[4096]{0:T(1024)} %param.16) | copy-start | bytes 49156
  11.2 26.9 %copy-start.9 = (s32[1,128,8]{1,2,0:T(8,128)S(1)}, s32[1,128,8]{1,2,0:T(8,128)}, u32[]{:S(2)}) copy-start(s32[1,128,8]{1,2,0:T(8,128)} %param.17) | copy-start | bytes 12292
  26.3 11.8 %collective-permute-start = (bf16[512,512]{1,0:T(8,128)(2,1)S(1)}, bf16[512,512]{1,0:T(8,128)(2,1)S(1)}, u32[]{:S(2)}, u32[]{:S(2)}) collective-permute-start(bf16[512,512]{1,0:T(8,128)(2,1)S(1)} %all_gather.6.own_k_ref.own_v_ref), channel_id=1, source_target_pairs={{0,128},{1,129},{2,130},{3,131},{4,132},{5,133},{6,134},{7,135},{8... | collective-permute-start | bytes 1572872 | tf_op jit(solution)/shard_map/ppermute | solution.py:457
  38.1 0.8 copy-start.6
  38.9 0.8 copy-start.7
  56.2 52.8 %copy-start.5 = (bf16[256,1536]{1,0:T(8,128)(2,1)}, bf16[256,1536]{1,0:T(8,128)(2,1)S(1)}, u32[]{:S(2)}) copy-start(bf16[256,1536]{1,0:T(8,128)(2,1)S(1)} %get-tuple-element.20) | copy-start | bytes 2359300
  109.0 42.2 %all-to-all-start.1 = ((bf16[32,8,1536]{2,1,0:T(8,128)(2,1)}), bf16[32,8,1536]{2,1,0:T(8,128)(2,1)S(1)}, u32[]{:S(2)}, u32[]{:S(2)}) async-start(bf16[32,8,1536]{2,1,0:T(8,128)(2,1)} %bitcast.42), calls=%async_computation.1 | async-start | bytes 1572864 | tf_op jit(solution)/shard_map/all_to_all | solution.py:477
  115.7 35.5 %collective-permute-start.1 = (bf16[768,512]{1,0:T(8,128)(2,1)}, bf16[768,512]{1,0:T(8,128)(2,1)}, u32[]{:S(2)}, u32[]{:S(2)}) collective-permute-start(bf16[768,512]{1,0:T(8,128)(2,1)} %get-tuple-element.32.refs_0_), channel_id=1, source_target_pairs={{0,32},{32,64},{64,96},{96,0},{1,33},{33,65},{65,97},{97,1},{2,34}... | collective-permute-start | bytes 2359304 | tf_op jit(solution)/shard_map/ppermute | solution.py:430
  115.7 64.4 %collective-permute-start.3 = (bf16[256,3072]{1,0:T(8,128)(2,1)S(1)}, bf16[256,3072]{1,0:T(8,128)(2,1)}, u32[]{:S(2)}, u32[]{:S(2)}) collective-permute-start(bf16[256,3072]{1,0:T(8,128)(2,1)S(1)} %bitcast.35), channel_id=1, source_target_pairs={{0,128},{128,0},{1,129},{129,1},{2,130},{130,2},{3,131},{131,3},{4... | collective-permute-start | bytes 4718600 | tf_op jit(solution)/shard_map/ppermute | solution.py:426
  119.6 32.5 %collective-permute-start.2 = (bf16[768,512]{1,0:T(8,128)(2,1)S(1)}, bf16[768,512]{1,0:T(8,128)(2,1)}, u32[]{:S(2)}, u32[]{:S(2)}) collective-permute-start(bf16[768,512]{1,0:T(8,128)(2,1)S(1)} %get-tuple-element.31.refs_1_), channel_id=1, source_target_pairs={{0,96},{32,0},{64,32},{96,64},{1,97},{33,1},{65,33},{97,65},{2,98}... | collective-permute-start | bytes 2359304 | tf_op jit(solution)/shard_map/ppermute | solution.py:430
  122.3 45.8 %collective-permute-start.6 = (bf16[768,512]{1,0:T(8,128)(2,1)S(1)}, bf16[768,512]{1,0:T(8,128)(2,1)}, u32[]{:S(2)}, u32[]{:S(2)}) collective-permute-start(bf16[768,512]{1,0:T(8,128)(2,1)S(1)} %get-tuple-element.31.refs_1_), channel_id=1, source_target_pairs={{0,32},{32,64},{64,96},{96,0},{1,33},{33,65},{65,97},{97,1},{2,34}... | collective-permute-start | bytes 2359304 | tf_op jit(solution)/shard_map/ppermute | solution.py:430
  122.3 46.3 %collective-permute-start.7 = (bf16[768,512]{1,0:T(8,128)(2,1)}, bf16[768,512]{1,0:T(8,128)(2,1)}, u32[]{:S(2)}, u32[]{:S(2)}) collective-permute-start(bf16[768,512]{1,0:T(8,128)(2,1)} %get-tuple-element.32.refs_0_), channel_id=1, source_target_pairs={{0,96},{32,0},{64,32},{96,64},{1,97},{33,1},{65,33},{97,65},{2,98}... | collective-permute-start | bytes 2359304 | tf_op jit(solution)/shard_map/ppermute | solution.py:430
  151.2 19.5 %collective-permute-start.4 = (bf16[256,1536]{1,0:T(8,128)(2,1)S(1)}, bf16[256,1536]{1,0:T(8,128)(2,1)}, u32[]{:S(2)}, u32[]{:S(2)}) collective-permute-start(bf16[256,1536]{1,0:T(8,128)(2,1)S(1)} %bitcast.37), channel_id=1, source_target_pairs={{0,128},{128,0},{1,129},{129,1},{2,130},{130,2},{3,131},{131,3},{4... | collective-permute-start | bytes 2359304 | tf_op jit(solution)/shard_map/ppermute | solution.py:426
  152.1 4.6 %copy-start = (bf16[16384,384]{1,0:T(8,128)(2,1)S(1)}, bf16[16384,384]{1,0:T(8,128)(2,1)}, u32[]{:S(2)}) copy-start(bf16[16384,384]{1,0:T(8,128)(2,1)} %all-gather.2.cloned.1.call-done) | copy-start | bytes 37748740
  156.7 23.4 %copy-start.1 = (bf16[16384,384]{1,0:T(8,128)(2,1)S(1)}, bf16[16384,384]{1,0:T(8,128)(2,1)}, u32[]{:S(2)}) copy-start(bf16[16384,384]{1,0:T(8,128)(2,1)} %all-gather.2.cloned.1.call-done) | copy-start | bytes 37748740
  163.5 16.6 %collective-permute-start.5 = (bf16[288,768]{1,0:T(8,128)(2,1)S(1)}, bf16[288,768]{1,0:T(8,128)(2,1)S(1)}, u32[]{:S(2)}, u32[]{:S(2)}) collective-permute-start(bf16[288,768]{1,0:T(8,128)(2,1)S(1)} %gate_up.2.own_a), channel_id=1, source_target_pairs={{0,128},{128,0},{1,129},{129,1},{2,130},{130,2},{3,131},{131,3},{4... | collective-permute-start | bytes 1327112 | tf_op jit(solution)/shard_map/ppermute | solution.py:426
  168.1 22.0 %collective-permute-start.9 = (bf16[768,512]{1,0:T(8,128)(2,1)}, bf16[768,512]{1,0:T(8,128)(2,1)S(1)}, u32[]{:S(2)}, u32[]{:S(2)}) collective-permute-start(bf16[768,512]{1,0:T(8,128)(2,1)} %collective-permute-done.1.refs_2_), channel_id=1, source_target_pairs={{0,32},{32,64},{64,96},{96,0},{1,33},{33,65},{65,97},{97,1},{2,34}... | collective-permute-start | bytes 2359304 | tf_op jit(solution)/shard_map/ppermute | solution.py:430
  168.6 21.4 %collective-permute-start.10 = (bf16[768,512]{1,0:T(8,128)(2,1)}, bf16[768,512]{1,0:T(8,128)(2,1)S(1)}, u32[]{:S(2)}, u32[]{:S(2)}) collective-permute-start(bf16[768,512]{1,0:T(8,128)(2,1)} %collective-permute-done.2.refs_5_), channel_id=1, source_target_pairs={{0,96},{32,0},{64,32},{96,64},{1,97},{33,1},{65,33},{97,65},{2,98}... | collective-permute-start | bytes 2359304 | tf_op jit(solution)/shard_map/ppermute | solution.py:430
  188.5 10.6 %collective-permute-start.8 = (bf16[288,768]{1,0:T(8,128)(2,1)S(1)}, bf16[288,768]{1,0:T(8,128)(2,1)S(1)}, u32[]{:S(2)}, u32[]{:S(2)}) collective-permute-start(bf16[288,768]{1,0:T(8,128)(2,1)S(1)} %gate_up.3.far_a), channel_id=1, source_target_pairs={{0,128},{128,0},{1,129},{129,1},{2,130},{130,2},{3,131},{131,3},{4... | collective-permute-start | bytes 1327112 | tf_op jit(solution)/shard_map/ppermute | solution.py:426
  209.2 12.4 %copy-start.10 = (f32[1,128,8]{1,2,0:T(8,128)S(1)}, f32[1,128,8]{1,2,0:T(8,128)}, u32[]{:S(2)}) copy-start(f32[1,128,8]{1,2,0:T(8,128)} %param.18) | copy-start | bytes 12292
  209.2 69.0 %all-to-all-start.2 = ((bf16[64,8,2304]{2,1,0:T(8,128)(2,1)}), bf16[64,8,2304]{2,1,0:T(8,128)(2,1)S(1)}, u32[]{:S(2)}, u32[]{:S(2)}) async-start(bf16[64,8,2304]{2,1,0:T(8,128)(2,1)} %bitcast.24), calls=%async_computation.2 | async-start | bytes 4718592 | tf_op jit(solution)/shard_map/all_to_all | solution.py:502
  278.2 1.6 copy-start.2
Sparse Core Ops, SparseCore 0:
  11.3 137.5 all-gather.1

commit v4 on v2

--- a/solution.py
+++ b/solution.py
@@ -459,10 +459,6 @@
     both = pack_weights(w_gate[0].T, w_up[0].T)
     both = lax.all_gather(both, "x", axis=0, tiled=True).reshape(4, width, both.shape[1])
     hidden, cols = w_down.shape[1:]
-    here = (w_down[0, : hidden // 2], w_down[0, hidden // 2 :])
-    left_top, right_bottom = ring(here[0], 1), ring(here[1], -1)
-    left_bottom, right_top = ring(here[1], 1), ring(here[0], -1)
-
     h_state, one, two = attend(
         place, queries[0], own_kv, far_kv, cos2, sin2, residual[0], norm_gain[None],
         expert_ids[0].T, owners,
@@ -486,15 +482,17 @@
     one = dispatch(one)
     far_one = swap(one)
     two = dispatch(two)
+    two, lower = lax.optimization_barrier((two, w_down[0]))
     far_two = swap(two)
-    early, left_top, right_bottom = lax.optimization_barrier((two, left_top, right_bottom))
-    own_a = gate_up(one, early, both)
-    own_a, left_top, right_bottom = lax.optimization_barrier((own_a, left_top, right_bottom))
+    here = (lower[: hidden // 2], lower[hidden // 2 :])
+    left_top, right_bottom = ring(here[0], 1), ring(here[1], -1)
+    left_bottom, right_top = ring(here[1], 1), ring(here[0], -1)
+    own_a = gate_up(one, two, both)
     far_b = swap(own_a)
+    far_two, far_b, left_top, right_bottom, left_bottom, right_top = lax.optimization_barrier(
+        (far_two, far_b, left_top, right_bottom, left_bottom, right_top)
+    )
     beyond = (ring(left_top, 1), ring(right_bottom, -1))
-    far_two, far_b, left_bottom, right_top = lax.optimization_barrier(
-        (far_two, far_b, left_bottom, right_top)
-    )
     far_a = gate_up(far_one, far_two, both)
     own_b = swap(far_a)
     lower = (*here, left_top, left_bottom, right_top, right_bottom, *beyond)

time: 289 us -> 310 us (1.073)
  waiting for transfers between devices: 117 us -> 153 us
  starting transfers between devices: 33.9 us -> 25.4 us
  blocking collectives: 59 us -> 52.9 us
    ppermute x4, waiting for transfers between devices: 15.7 us -> 34.3 us  [swap(): return lax.ppermute(x, 'y', [(0, 1), (1, 0)])]
    all_to_all x1, waiting for transfers between devices: 19.7 us -> 31.4 us  [dispatch(): lax.all_to_all(rows.reshape(owners, MAIN, wide), ('y', 'exp'), split_axis...]
    all_gather x1, waiting for transfers between devices: 6 us -> 14 us  [per_device(): lax.all_gather(both, 'x', axis=0, tiled=True)]
    all_to_all x1, blocking collectives: 47.3 us -> 41.2 us  [dispatch(): lax.all_to_all(rows.reshape(owners, MAIN, wide), ('y', 'exp'), split_axis...]
    ppermute x4, starting transfers between devices: 9.49 us -> 5.05 us  [swap(): return lax.ppermute(x, 'y', [(0, 1), (1, 0)])]
    all_to_all x1, starting transfers between devices: 11.9 us -> 8.53 us  [per_device(): lax.all_to_all(out.reshape(2 * owners, MAIN, out.shape[2]), ('y', 'exp'),...]
    unnamed x24 -> x28, local copies, waits for them, and re-layouts: 8.65 us -> 8.66 us
  transfers between devices with their start and end apart: 14 -> 14, of which waited for: 9 -> 9; matrix products, arithmetic and copies ran while one was open for 1% -> 1% of each run, Pallas kernels for 12% -> 11%
where the time goes in v4:
time: 310 us; the launch traced here: 309 us
  waiting for transfers between devices  153 us (49%)
  blocking collectives  52.9 us (17%)
  Pallas kernels  51.8 us (17%)
  starting transfers between devices  25.4 us (8%)
  between operations  13.5 us (4%)
  local copies, waits for them, and re-layouts  11 us (4%)
    all_to_all x1, waiting for transfers between devices, per_device(): lax.all_to_all(out.reshape(2 * owners, MAIN, out.shape[2]), ('y', 'exp'),...  56.4 us
    all_to_all x1, blocking collectives, dispatch(): lax.all_to_all(rows.reshape(owners, MAIN, wide), ('y', 'exp'), split_axis...  41.2 us
    ppermute x4, waiting for transfers between devices, swap(): return lax.ppermute(x, 'y', [(0, 1), (1, 0)])  34.3 us
    all_to_all x1, waiting for transfers between devices, dispatch(): lax.all_to_all(rows.reshape(owners, MAIN, wide), ('y', 'exp'), split_axis...  31.4 us
    pallas_call x1, Pallas kernels, attend(): pl.pallas_call(attend_kernel, grid_spec=pltpu.PrefetchScalarGridSpec(num_...  16.5 us
    pallas_call x2, Pallas kernels, gate_up(): pl.pallas_call(gate_up_kernel, grid=(shards,), in_specs=[pl.BlockSpec(one...  15.1 us
    all_gather x1, waiting for transfers between devices, per_device(): lax.all_gather(both, 'x', axis=0, tiled=True)  14 us
    all_gather x1, blocking collectives, per_device(): own_kv = lax.all_gather(kv, 'x', axis=0, tiled=True)  11.7 us
  transfers between devices with their start and end apart: 14, of which 9 were waited for; matrix products, arithmetic and copies ran while one was open for 1% of the time, Pallas kernels for 11%

profile of v4, /device:TPU:17, one launch (start us, length us, event | category | flops | bytes accessed | tf_op | source)
XLA Modules:
  0.0 309.1 jit_solution(6009339790430461720)
XLA Ops:
  6.5 4.6 %pack_weights.1 = bf16[4096,384]{1,0:T(8,128)(2,1)} custom-call(bf16[192,4096]{1,0:T(8,128)(2,1)} %bitcast.45, bf16[192,4096]{1,0:T(8,128)(2,1)} %bitcast.46), custom_call_target="tpu_custom_call" | custom-call | tf_op jit(solution)/shard_map/pack_weights/pallas_call | solution.py:89
  11.2 0.0 all-gather.2.cloned.1.call-update
  11.2 0.0 copy-start.5
  11.2 0.0 copy-start.9
  11.2 0.0 copy-start.10
  11.2 0.6 copy-done.12
  11.8 0.3 fusion.2
  12.1 0.8 pad_maximum_fusion
  12.9 1.7 pack_kv.1
  14.6 11.7 %all_gather.6.own_k_ref.own_v_ref = bf16[512,512]{1,0:T(8,128)(2,1)S(1)} all-gather(bf16[128,512]{1,0:T(8,128)(2,1)} %pack_kv.1), channel_id=1, replica_groups=mesh['y'=2,'x'=4,'exp'=32] {'x'}, dimensions={0}, use_global_device_ids=true | all-gather | bytes 655360 | tf_op jit(solution)/shard_map/all_gather | solution.py:456
  26.3 2.9 collective-permute-start
  29.2 0.1 pad_add_fusion.place_ref
  29.3 8.8 %collective-permute-done.far_k_ref.far_v_ref = bf16[512,512]{1,0:T(8,128)(2,1)S(1)} collective-permute-done((bf16[512,512]{1,0:T(8,128)(2,1)S(1)}, bf16[512,512]{1,0:T(8,128)(2,1)S(1)}, u32[]{:S(2)}, u32[]{:S(2)}) %collective-permute-start) | collective-permute-done | bytes 524320 | tf_op jit(solution)/shard_map/ppermute | solution.py:457
  38.1 0.8 copy-done.7
  38.9 0.8 copy-done.8
  39.8 16.5 %attend.1 = (f32[128,4096]{1,0:T(8,128)}, bf16[256,2560]{1,0:T(8,128)(2,1)S(1)}, bf16[256,2048]{1,0:T(8,128)(2,1)S(1)}) custom-call(s32[3]{0:T(128)S(1)} %pad_add_fusion.place_ref, bf16[128,4096]{1,0:T(8,128)(2,1)S(1)} %bitcast.38, bf16[512,512]{1,0:T(8,128)(2,1)S(1)} %all_gather.6.own_k_ref.own_v_ref, bf16[512,512]{1,0:T(8,128)(2,1)S(1)} %all_gather.6.own_k_ref.own_v_ref, ...), custom_call_target="tpu_custom_call" | custom-call | tf_op jit(solution)/shard_map/attend/pallas_call | solution.py:186
  56.3 41.2 %all_to_all.15 = bf16[32,8,2048]{2,1,0:T(8,128)(2,1)S(1)} all-to-all(bf16[32,8,2048]{2,1,0:T(8,128)(2,1)S(1)} %bitcast.37), channel_id=1, replica_groups={{0,1,130,131,4,5,134,135,8,9,138,139,12,13,142,143,16,17,146,147,20,21,..., dimensions={0} | all-to-all | bytes 2097152 | tf_op jit(solution)/shard_map/all_to_all | solution.py:473
  97.5 4.7 %all-to-all-start = ((bf16[32,8,2560]{2,1,0:T(8,128)(2,1)}), bf16[32,8,2560]{2,1,0:T(8,128)(2,1)S(1)}, u32[]{:S(2)}, u32[]{:S(2)}) async-start(bf16[32,8,2560]{2,1,0:T(8,128)(2,1)} %bitcast.36), calls=%async_computation | async-start | bytes 2621440 | tf_op jit(solution)/shard_map/all_to_all | solution.py:473
  102.2 2.4 fusion.8
  104.6 0.0 collective-permute-start.6
  104.6 31.4 %all-to-all-done = bf16[32,8,2560]{2,1,0:T(8,128)(2,1)S(1)} async-done(((bf16[32,8,2560]{2,1,0:T(8,128)(2,1)}), bf16[32,8,2560]{2,1,0:T(8,128)(2,1)S(1)}, u32[]{:S(2)}, u32[]{:S(2)}) %all-to-all-start) | async-done | bytes 1310752 | tf_op jit(solution)/shard_map/all_to_all | solution.py:473
  135.9 3.7 %collective-permute-start.1 = (bf16[256,2560]{1,0:T(8,128)(2,1)S(1)}, bf16[256,2560]{1,0:T(8,128)(2,1)}, u32[]{:S(2)}, u32[]{:S(2)}) collective-permute-start(bf16[256,2560]{1,0:T(8,128)(2,1)S(1)} %bitcast.32), channel_id=1, source_target_pairs={{0,128},{128,0},{1,129},{129,1},{2,130},{130,2},{3,131},{131,3},{4... | collective-permute-start | bytes 3932168 | tf_op jit(solution)/shard_map/ppermute | solution.py:426
  139.7 0.9 collective-permute-start.5
  140.6 0.6 collective-permute-start.7
  141.1 0.8 collective-permute-done.6.refs_3_
  142.0 0.0 collective-permute-start.4
  142.0 14.0 %all-gather.2.cloned.1.call-done = bf16[16384,384]{1,0:T(8,128)(2,1)} async-done(((bf16[4096,384]{1,0:T(8,128)(2,1)}), bf16[16384,384]{1,0:T(8,128)(2,1)}) %all-gather.2.cloned.1.call-update) | async-done | bytes 12582928 | tf_op jit(solution)/shard_map/all_gather | solution.py:460
  156.0 4.6 %copy-done = bf16[16384,384]{1,0:T(8,128)(2,1)S(1)} copy-done((bf16[16384,384]{1,0:T(8,128)(2,1)S(1)}, bf16[16384,384]{1,0:T(8,128)(2,1)}, u32[]{:S(2)}) %copy-start) | copy-done | bytes 12582936
  160.6 6.7 %gate_up.2.own_a = bf16[288,768]{1,0:T(8,128)(2,1)S(1)} custom-call(bf16[256,2560]{1,0:T(8,128)(2,1)S(1)} %bitcast.33, bf16[256,2048]{1,0:T(8,128)(2,1)S(1)} %bitcast.35, bf16[4,4096,384]{2,1,0:T(8,128)(2,1)S(1)} %bitcast.29), custom_call_target="tpu_custom_call" | custom-call | flops 3623878656 | bytes 14942208 | tf_op jit(solution)/shard_map/gate_up/pallas_call | solution.py:262
  167.3 0.0 copy-start.2
  167.3 0.0 collective-permute-done.5.refs_5_
  167.3 0.1 collective-permute-start.3
  167.4 7.5 %collective-permute-done.7.refs_4_ = bf16[768,512]{1,0:T(8,128)(2,1)} collective-permute-done((bf16[768,512]{1,0:T(8,128)(2,1)}, bf16[768,512]{1,0:T(8,128)(2,1)}, u32[]{:S(2)}, u32[]{:S(2)}) %collective-permute-start.7) | collective-permute-done | bytes 786464 | tf_op jit(solution)/shard_map/ppermute | solution.py:430
  174.9 0.0 collective-permute-done.4.refs_2_
  174.9 16.0 %collective-permute-done.2.two_ref = bf16[256,2048]{1,0:T(8,128)(2,1)} collective-permute-done((bf16[256,2048]{1,0:T(8,128)(2,1)S(1)}, bf16[256,2048]{1,0:T(8,128)(2,1)}, u32[]{:S(2)}, u32[]{:S(2)}) %collective-permute-start.2) | collective-permute-done | bytes 1048608 | tf_op jit(solution)/shard_map/ppermute | solution.py:426
  191.0 9.4 %collective-permute-done.3.far_b = bf16[288,768]{1,0:T(8,128)(2,1)S(1)} collective-permute-done((bf16[288,768]{1,0:T(8,128)(2,1)S(1)}, bf16[288,768]{1,0:T(8,128)(2,1)S(1)}, u32[]{:S(2)}, u32[]{:S(2)}) %collective-permute-start.3) | collective-permute-done | bytes 442400 | tf_op jit(solution)/shard_map/ppermute | solution.py:426
  200.3 2.7 collective-permute-start.10
  203.0 0.0 collective-permute-done.1.one_ref
  203.0 8.4 %gate_up.3.far_a = bf16[288,768]{1,0:T(8,128)(2,1)S(1)} custom-call(bf16[256,2560]{1,0:T(8,128)(2,1)} %collective-permute-done.1.one_ref, bf16[256,2048]{1,0:T(8,128)(2,1)} %collective-permute-done.2.two_ref, bf16[4,4096,384]{2,1,0:T(8,128)(2,1)S(1)} %bitcast.30), custom_call_target="tpu_custom_call" | custom-call | flops 3623878656 | bytes 14942208 | tf_op jit(solution)/shard_map/gate_up/pallas_call | solution.py:262
  211.4 1.2 collective-permute-start.8
  212.6 8.9 %collective-permute-done.8.own_b = bf16[288,768]{1,0:T(8,128)(2,1)S(1)} collective-permute-done((bf16[288,768]{1,0:T(8,128)(2,1)S(1)}, bf16[288,768]{1,0:T(8,128)(2,1)S(1)}, u32[]{:S(2)}, u32[]{:S(2)}) %collective-permute-start.8) | collective-permute-done | bytes 442400 | tf_op jit(solution)/shard_map/ppermute | solution.py:426
  221.6 9.9 %down.1 = bf16[2,256,2304]{2,1,0:T(8,128)(2,1)} custom-call(s32[3]{0:T(128)S(1)} %pad_add_fusion.place_ref, bf16[288,768]{1,0:T(8,128)(2,1)S(1)} %gate_up.2.own_a, bf16[288,768]{1,0:T(8,128)(2,1)S(1)} %collective-permute-done.8.own_b, bf16[288,768]{1,0:T(8,128)(2,1)S(1)} %gate_up.3.far_a, bf16[288,768]{1,0:T(8,128)(2,1)S(1)} %collective-permute-done.3.far_b, ...), custom_call_target="tpu_custom_call" | custom-call | tf_op jit(solution)/shard_map/down/pallas_call | solution.py:346
  231.5 8.5 %all-to-all-start.2 = ((bf16[64,8,2304]{2,1,0:T(8,128)(2,1)}), bf16[64,8,2304]{2,1,0:T(8,128)(2,1)S(1)}, u32[]{:S(2)}, u32[]{:S(2)}) async-start(bf16[64,8,2304]{2,1,0:T(8,128)(2,1)} %bitcast.23), calls=%async_computation.2 | async-start | bytes 4718592 | tf_op jit(solution)/shard_map/all_to_all | solution.py:500
  240.0 0.1 copy.12
  240.1 0.1 copy.13
  240.2 56.4 %all-to-all-done.2 = bf16[64,8,2304]{2,1,0:T(8,128)(2,1)S(1)} async-done(((bf16[64,8,2304]{2,1,0:T(8,128)(2,1)}), bf16[64,8,2304]{2,1,0:T(8,128)(2,1)S(1)}, u32[]{:S(2)}, u32[]{:S(2)}) %all-to-all-start.2) | async-done | bytes 2359328 | tf_op jit(solution)/shard_map/all_to_all | solution.py:500
  296.7 1.6 copy-done.3
  298.3 4.0 %combine.1 = bf16[128,4096]{1,0:T(8,128)(2,1)} custom-call(s32[128,8]{1,0:T(8,128)S(1)} %bitcast.40, f32[128,8]{1,0:T(8,128)S(1)} %bitcast.41, f32[128,4096]{1,0:T(8,128)S(1)} %copy-done.3, bf16[2,256,2304]{2,1,0:T(8,128)(2,1)S(1)} %bitcast.31), custom_call_target="tpu_custom_call" | custom-call | tf_op jit(solution)/shard_map/combine/pallas_call | solution.py:409
  (24 shorter events, 0.1 us)
Async XLA Ops:
  6.5 149.4 %all-gather.2.cloned.1.call-start = ((), (), s32[]{:S(2)}) async-start(), calls=%async_computation.3 | async-start | bytes 15728640 | tf_op jit(solution)/shard_map/all_gather | solution.py:460
  11.1 0.7 copy-start.12
  11.1 26.9 %copy-start.6 = (bf16[1,128,4096]{2,1,0:T(8,128)(2,1)S(1)}, bf16[1,128,4096]{2,1,0:T(8,128)(2,1)}, u32[]{:S(2)}) copy-start(bf16[1,128,4096]{2,1,0:T(8,128)(2,1)} %param.15) | copy-start | bytes 3145732
  11.2 26.9 %copy-start.5 = (bf16[1,128,4096]{2,1,0:T(8,128)(2,1)S(1)}, bf16[1,128,4096]{2,1,0:T(8,128)(2,1)}, u32[]{:S(2)}) copy-start(bf16[1,128,4096]{2,1,0:T(8,128)(2,1)} %param.11) | copy-start | bytes 3145732
  11.2 26.9 %copy-start.9 = (f32[4096]{0:T(1024)S(1)}, f32[4096]{0:T(1024)}, u32[]{:S(2)}) copy-start(f32[4096]{0:T(1024)} %param.16) | copy-start | bytes 49156
  11.2 26.9 %copy-start.10 = (s32[1,128,8]{1,2,0:T(8,128)S(1)}, s32[1,128,8]{1,2,0:T(8,128)}, u32[]{:S(2)}) copy-start(s32[1,128,8]{1,2,0:T(8,128)} %param.17) | copy-start | bytes 12292
  26.3 11.8 %collective-permute-start = (bf16[512,512]{1,0:T(8,128)(2,1)S(1)}, bf16[512,512]{1,0:T(8,128)(2,1)S(1)}, u32[]{:S(2)}, u32[]{:S(2)}) collective-permute-start(bf16[512,512]{1,0:T(8,128)(2,1)S(1)} %all_gather.6.own_k_ref.own_v_ref), channel_id=1, source_target_pairs={{0,128},{1,129},{2,130},{3,131},{4,132},{5,133},{6,134},{7,135},{8... | collective-permute-start | bytes 1572872 | tf_op jit(solution)/shard_map/ppermute | solution.py:457
  38.1 0.8 copy-start.7
  38.9 0.8 copy-start.8
  56.3 41.2 %copy-start.4 = (bf16[256,2560]{1,0:T(8,128)(2,1)}, bf16[256,2560]{1,0:T(8,128)(2,1)S(1)}, u32[]{:S(2)}) copy-start(bf16[256,2560]{1,0:T(8,128)(2,1)S(1)} %get-tuple-element.17) | copy-start | bytes 3932164
  97.5 38.5 %all-to-all-start = ((bf16[32,8,2560]{2,1,0:T(8,128)(2,1)}), bf16[32,8,2560]{2,1,0:T(8,128)(2,1)S(1)}, u32[]{:S(2)}, u32[]{:S(2)}) async-start(bf16[32,8,2560]{2,1,0:T(8,128)(2,1)} %bitcast.36), calls=%async_computation | async-start | bytes 2621440 | tf_op jit(solution)/shard_map/all_to_all | solution.py:473
  104.6 37.4 %collective-permute-start.6 = (bf16[768,512]{1,0:T(8,128)(2,1)S(1)}, bf16[768,512]{1,0:T(8,128)(2,1)}, u32[]{:S(2)}, u32[]{:S(2)}) collective-permute-start(bf16[768,512]{1,0:T(8,128)(2,1)S(1)} %get-tuple-element.27.refs_1_), channel_id=1, source_target_pairs={{0,32},{32,64},{64,96},{96,0},{1,33},{33,65},{65,97},{97,1},{2,34}... | collective-permute-start | bytes 2359304 | tf_op jit(solution)/shard_map/ppermute | solution.py:430
  135.9 67.1 %collective-permute-start.1 = (bf16[256,2560]{1,0:T(8,128)(2,1)S(1)}, bf16[256,2560]{1,0:T(8,128)(2,1)}, u32[]{:S(2)}, u32[]{:S(2)}) collective-permute-start(bf16[256,2560]{1,0:T(8,128)(2,1)S(1)} %bitcast.32), channel_id=1, source_target_pairs={{0,128},{128,0},{1,129},{129,1},{2,130},{130,2},{3,131},{131,3},{4... | collective-permute-start | bytes 3932168 | tf_op jit(solution)/shard_map/ppermute | solution.py:426
  139.7 27.6 %collective-permute-start.5 = (bf16[768,512]{1,0:T(8,128)(2,1)S(1)}, bf16[768,512]{1,0:T(8,128)(2,1)}, u32[]{:S(2)}, u32[]{:S(2)}) collective-permute-start(bf16[768,512]{1,0:T(8,128)(2,1)S(1)} %get-tuple-element.27.refs_1_), channel_id=1, source_target_pairs={{0,96},{32,0},{64,32},{96,64},{1,97},{33,1},{65,33},{97,65},{2,98}... | collective-permute-start | bytes 2359304 | tf_op jit(solution)/shard_map/ppermute | solution.py:430
  140.6 50.4 %collective-permute-start.2 = (bf16[256,2048]{1,0:T(8,128)(2,1)S(1)}, bf16[256,2048]{1,0:T(8,128)(2,1)}, u32[]{:S(2)}, u32[]{:S(2)}) collective-permute-start(bf16[256,2048]{1,0:T(8,128)(2,1)S(1)} %bitcast.34), channel_id=1, source_target_pairs={{0,128},{128,0},{1,129},{129,1},{2,130},{130,2},{3,131},{131,3},{4... | collective-permute-start | bytes 3145736 | tf_op jit(solution)/shard_map/ppermute | solution.py:426
  140.6 34.4 %collective-permute-start.7 = (bf16[768,512]{1,0:T(8,128)(2,1)}, bf16[768,512]{1,0:T(8,128)(2,1)}, u32[]{:S(2)}, u32[]{:S(2)}) collective-permute-start(bf16[768,512]{1,0:T(8,128)(2,1)} %get-tuple-element.28.refs_0_), channel_id=1, source_target_pairs={{0,96},{32,0},{64,32},{96,64},{1,97},{33,1},{65,33},{97,65},{2,98}... | collective-permute-start | bytes 2359304 | tf_op jit(solution)/shard_map/ppermute | solution.py:430
  142.0 33.0 %collective-permute-start.4 = (bf16[768,512]{1,0:T(8,128)(2,1)}, bf16[768,512]{1,0:T(8,128)(2,1)}, u32[]{:S(2)}, u32[]{:S(2)}) collective-permute-start(bf16[768,512]{1,0:T(8,128)(2,1)} %get-tuple-element.28.refs_0_), channel_id=1, source_target_pairs={{0,32},{32,64},{64,96},{96,0},{1,33},{33,65},{65,97},{97,1},{2,34}... | collective-permute-start | bytes 2359304 | tf_op jit(solution)/shard_map/ppermute | solution.py:430
  156.0 4.6 %copy-start = (bf16[16384,384]{1,0:T(8,128)(2,1)S(1)}, bf16[16384,384]{1,0:T(8,128)(2,1)}, u32[]{:S(2)}) copy-start(bf16[16384,384]{1,0:T(8,128)(2,1)} %all-gather.2.cloned.1.call-done) | copy-start | bytes 37748740
  160.6 42.5 %copy-start.1 = (bf16[16384,384]{1,0:T(8,128)(2,1)S(1)}, bf16[16384,384]{1,0:T(8,128)(2,1)}, u32[]{:S(2)}) copy-start(bf16[16384,384]{1,0:T(8,128)(2,1)} %all-gather.2.cloned.1.call-done) | copy-start | bytes 37748740
  167.3 54.3 %copy-start.2 = (bf16[768,512]{1,0:T(8,128)(2,1)S(1)}, bf16[768,512]{1,0:T(8,128)(2,1)}, u32[]{:S(2)}) copy-start(bf16[768,512]{1,0:T(8,128)(2,1)} %get-tuple-element.28.refs_0_) | copy-start | bytes 2359300
  167.3 33.0 %collective-permute-start.3 = (bf16[288,768]{1,0:T(8,128)(2,1)S(1)}, bf16[288,768]{1,0:T(8,128)(2,1)S(1)}, u32[]{:S(2)}, u32[]{:S(2)}) collective-permute-start(bf16[288,768]{1,0:T(8,128)(2,1)S(1)} %gate_up.2.own_a), channel_id=1, source_target_pairs={{0,128},{128,0},{1,129},{129,1},{2,130},{130,2},{3,131},{131,3},{4... | collective-permute-start | bytes 1327112 | tf_op jit(solution)/shard_map/ppermute | solution.py:426
  200.3 21.2 %collective-permute-start.9 = (bf16[768,512]{1,0:T(8,128)(2,1)}, bf16[768,512]{1,0:T(8,128)(2,1)S(1)}, u32[]{:S(2)}, u32[]{:S(2)}) collective-permute-start(bf16[768,512]{1,0:T(8,128)(2,1)} %collective-permute-done.4.refs_2_), channel_id=1, source_target_pairs={{0,32},{32,64},{64,96},{96,0},{1,33},{33,65},{65,97},{97,1},{2,34}... | collective-permute-start | bytes 2359304 | tf_op jit(solution)/shard_map/ppermute | solution.py:430
  200.3 21.2 %collective-permute-start.10 = (bf16[768,512]{1,0:T(8,128)(2,1)}, bf16[768,512]{1,0:T(8,128)(2,1)S(1)}, u32[]{:S(2)}, u32[]{:S(2)}) collective-permute-start(bf16[768,512]{1,0:T(8,128)(2,1)} %collective-permute-done.5.refs_5_), channel_id=1, source_target_pairs={{0,96},{32,0},{64,32},{96,64},{1,97},{33,1},{65,33},{97,65},{2,98}... | collective-permute-start | bytes 2359304 | tf_op jit(solution)/shard_map/ppermute | solution.py:430
  211.4 10.2 %collective-permute-start.8 = (bf16[288,768]{1,0:T(8,128)(2,1)S(1)}, bf16[288,768]{1,0:T(8,128)(2,1)S(1)}, u32[]{:S(2)}, u32[]{:S(2)}) collective-permute-start(bf16[288,768]{1,0:T(8,128)(2,1)S(1)} %gate_up.3.far_a), channel_id=1, source_target_pairs={{0,128},{128,0},{1,129},{129,1},{2,130},{130,2},{3,131},{131,3},{4... | collective-permute-start | bytes 1327112 | tf_op jit(solution)/shard_map/ppermute | solution.py:426
  231.5 8.6 %copy-start.11 = (f32[1,128,8]{1,2,0:T(8,128)S(1)}, f32[1,128,8]{1,2,0:T(8,128)}, u32[]{:S(2)}) copy-start(f32[1,128,8]{1,2,0:T(8,128)} %param.18) | copy-start | bytes 12292
  231.5 65.2 %all-to-all-start.2 = ((bf16[64,8,2304]{2,1,0:T(8,128)(2,1)}), bf16[64,8,2304]{2,1,0:T(8,128)(2,1)S(1)}, u32[]{:S(2)}, u32[]{:S(2)}) async-start(bf16[64,8,2304]{2,1,0:T(8,128)(2,1)} %bitcast.23), calls=%async_computation.2 | async-start | bytes 4718592 | tf_op jit(solution)/shard_map/all_to_all | solution.py:500
  296.7 1.6 copy-start.3
Sparse Core Ops, SparseCore 0:
  11.3 144.6 all-gather.1
